TPU v7x, 32 devices: a whole 2x2x4 slice. The times are simulated.
32 devices in a mesh: dp: 16 (over z, x, core), mp: 2 (over y).
Axes of the slice: x: 2, y: 2, z: 4, core: 2. Of those that a mesh axis runs over, the one named last changes fastest.
Arguments:
- tokens: bfloat16 [8192, 768], P('dp'), may hold values from -6 to 6
- gain_attn: bfloat16 [768], replicated, may hold values from 0.5 to 1.5
- w_query: bfloat16 [768, 768], P(None, 'mp'), may hold values from -0.0546875 to 0.0546875
- w_key: bfloat16 [768, 768], P(None, 'mp'), may hold values from -0.21875 to 0.21875
- w_value: bfloat16 [768, 768], P(None, 'mp'), may hold values from -0.21875 to 0.21875
- w_output: bfloat16 [768, 768], P('mp'), may hold values from -0.625 to 0.625
- position_table: bfloat16 [32, 12], P(None, 'mp'), may hold values from -5 to 5
- gain_moe: bfloat16 [768], replicated, may hold values from 0.5 to 1.5
- w_router: bfloat16 [768, 4], replicated, may hold values from -0.15625 to 0.15625
- w_in: bfloat16 [4, 768, 3072], P(None, None, 'mp'), may hold values from -0.21875 to 0.21875
- w_out: bfloat16 [4, 3072, 768], P(None, 'mp'), may hold values from -1.5 to 1.5
- cotangent: bfloat16 [8192, 768], P('dp'), may hold values from -6 to 6
- seq_lengths: int32 [16, 4], P('dp'), may hold values from 0 to 512, as said below
- expert_ids: int32 [8192], P('dp'), may hold values from 0 to 3, as said below
Outputs:
- mixed: bfloat16 [8192, 768], P('dp')
- grad_tokens: float32 [8192, 768], P('dp')
- grad_gain_attn: float32 [768], P('dp')
- grad_query: float32 [768, 768], P('dp', 'mp')
- grad_key: float32 [768, 768], P('dp', 'mp')
- grad_value: float32 [768, 768], P('dp', 'mp')
- grad_output: float32 [768, 768], P('mp', 'dp')
- grad_table: float32 [32, 12], P(None, 'mp')
- grad_gain_moe: float32 [768], P('dp')
- grad_router: float32 [768, 4], P('dp')
- grad_in: float32 [4, 768, 3072], P(None, 'dp', 'mp')
- grad_out: float32 [4, 3072, 768], P(None, 'mp', 'dp')
Inputs may be any that keep to these rules, and one draw needn't show every extreme that they name: `seq_lengths`: row b lists the lengths of the sequences that fill token batch b from its first slot on, in order, 0 for an unused entry; a row sums to 512 or less, the slots after it being padding; in every draw some row is one sequence of 512 tokens. `expert_ids`: in every token batch some expert is named by at least 160 of its 512 tokens.
All inputs are finite; a program needn't handle non-finite values.
Results may differ from a plain program's by a relative error of at most 0.017.
The roundings to bfloat16 on the way count: a program that leaves them out, or rounds other values in their place, can miss the bound.
Values sent between devices are 32-bit elements; how exact they have to be, the bound alone decides.
No kernel may reach another device: no remote copies, remote signals or barrier semaphores. Data moves between devices by JAX's collectives and lax.ppermute only.
A program may use at most 192 MiB of HBM per device.

v0:
```python
import jax
import jax.numpy as jnp
from jax import lax
from jax.sharding import PartitionSpec as P

HEAD = 64
NB = 32
E = 4
CAP = 160


EPS = 1e-06
THRESHOLDS = (12, 16, 23, 32, 46, 64, 91)


def layout(lengths, count):
    ends = jnp.cumsum(lengths)
    places = jnp.arange(count, dtype=jnp.int32)
    after = places[:, None] >= ends[None, :]
    segment = jnp.sum(after.astype(jnp.int32), axis=1)
    begin = jnp.sum(jnp.where(after, lengths[None, :], 0), axis=1)
    return (segment, places - begin)


def relative_bucket(query_pos, key_pos):
    offset = key_pos[None, :] - query_pos[:, None]
    distance = jnp.abs(offset)
    far_side = 8 + sum(((distance >= edge).astype(jnp.int32) for edge in THRESHOLDS))
    near = jnp.where(distance < 8, distance, far_side)
    return jnp.where(offset > 0, NB // 2, 0) + near


def capacity_slots(expert_ids):
    count = expert_ids.shape[0]
    chosen = (expert_ids[:, None] == jnp.arange(E, dtype=jnp.int32)[None, :]).astype(jnp.int32)
    before = jnp.cumsum(chosen, axis=0) - chosen
    rank = jnp.sum(before * chosen, axis=1)
    kept = rank < CAP
    flat = expert_ids * CAP + rank
    target = jnp.where(kept, flat, E * CAP)
    source = (
        jnp.zeros((E * CAP,), jnp.int32)
        .at[target]
        .set(jnp.arange(count, dtype=jnp.int32), mode="drop")
    )
    filled = jnp.zeros((E * CAP,), jnp.int32).at[target].set(1, mode="drop")
    return (kept, jnp.where(kept, flat, 0), source, filled, chosen)


def norm_rows(values, gain):
    return values * lax.rsqrt(jnp.mean(values * values, axis=-1, keepdims=True) + EPS) * gain


def shards(
    tokens,
    gain_attn,
    w_query,
    w_key,
    w_value,
    w_output,
    position_table,
    gain_moe,
    w_router,
    w_in,
    w_out,
    cotangent,
    seq_lengths,
    expert_ids,
):
    count = tokens.shape[0]
    heads = position_table.shape[1]
    inner = heads * HEAD
    block = min(512, count)
    starts = list(range(0, count, block))
    segment, position = layout(seq_lengths[0], count)
    kept, flat, source, filled, chosen = capacity_slots(expert_ids)
    keep_rows = kept.astype(jnp.float32)[:, None]
    slot_live = filled.astype(jnp.bfloat16)[:, None]
    picked = chosen.astype(jnp.float32)
    inputs = tokens.astype(jnp.float32)
    gain_one = gain_attn.astype(jnp.float32)
    gain_two = gain_moe.astype(jnp.float32)
    bucket_ids = jnp.arange(NB, dtype=jnp.int32)
    normed = norm_rows(inputs, gain_one).astype(jnp.bfloat16)
    query = (
        jnp.dot(normed, w_query, preferred_element_type=jnp.float32)
        .astype(jnp.bfloat16)
        .reshape(count, heads, HEAD)
    )
    keys = (
        jnp.dot(normed, w_key, preferred_element_type=jnp.float32)
        .astype(jnp.bfloat16)
        .reshape(count, heads, HEAD)
    )
    values = (
        jnp.dot(normed, w_value, preferred_element_type=jnp.float32)
        .astype(jnp.bfloat16)
        .reshape(count, heads, HEAD)
    )

    def block_scores():
        bucket = relative_bucket(position, position)
        onehot = (bucket[:, :, None] == bucket_ids[None, None, :]).astype(jnp.bfloat16)
        bias = jnp.einsum("qkb,bh->hqk", onehot, position_table, preferred_element_type=jnp.float32)
        scores = jnp.einsum("qhd,khd->hqk", query, keys, preferred_element_type=jnp.float32) + bias
        allowed = segment[:, None] == segment[None, :]
        return (jnp.where(allowed[None], scores, -1000000000.0), onehot, query)

    attended = []
    totals = []
    for begin in starts:
        scores, onehot, query_block = block_scores()
        peak = jnp.max(scores, axis=-1, keepdims=True)
        total = peak + jnp.log(jnp.sum(jnp.exp(scores - peak), axis=-1, keepdims=True))
        probs = jnp.exp(scores - total).astype(jnp.bfloat16)
        attended.append(
            jnp.einsum("hqk,khd->qhd", probs, values, preferred_element_type=jnp.float32)
        )
        totals.append(total)
    context = attended[0].reshape(count, inner).astype(jnp.bfloat16)
    partial_value = jnp.dot(context, w_output, preferred_element_type=jnp.float32)
    middle = inputs + lax.psum(partial_value, "mp")
    normed_two = norm_rows(middle, gain_two).astype(jnp.bfloat16)
    logits = jnp.dot(normed_two, w_router, preferred_element_type=jnp.float32)
    router = jax.nn.softmax(logits, axis=-1)
    gate = jnp.sum(router * picked, axis=1, keepdims=True)
    dispatch = (normed_two[source] * slot_live).reshape(E, CAP, -1)
    pre_act = jnp.einsum("ecd,edf->ecf", dispatch, w_in, preferred_element_type=jnp.float32)
    hidden = jax.nn.gelu(pre_act).astype(jnp.bfloat16)
    expert_part = jnp.einsum(
        "ecf,efd->ecd", hidden, w_out, preferred_element_type=jnp.float32
    ).reshape(E * CAP, -1)
    expert_full = lax.psum(expert_part[flat] * keep_rows, "mp")
    mixed = (middle + gate * expert_full).astype(jnp.bfloat16)
    grad_seed = cotangent.astype(jnp.float32)
    gate_grad = jnp.sum(grad_seed * expert_full, axis=1, keepdims=True)
    full_grad = (gate * grad_seed).astype(jnp.bfloat16)
    slot_grad = (full_grad[source] * slot_live).reshape(E, CAP, -1)
    grad_out_w = jnp.einsum("ecf,ecd->efd", hidden, slot_grad, preferred_element_type=jnp.float32)
    hidden_grad = jnp.einsum("ecd,efd->ecf", slot_grad, w_out, preferred_element_type=jnp.float32)
    _, gelu_pull = jax.vjp(jax.nn.gelu, pre_act)
    pre_grad = gelu_pull(hidden_grad)[0].astype(jnp.bfloat16)
    grad_in_w = jnp.einsum("ecd,ecf->edf", dispatch, pre_grad, preferred_element_type=jnp.float32)
    back_part = jnp.einsum(
        "ecf,edf->ecd", pre_grad, w_in, preferred_element_type=jnp.float32
    ).reshape(E * CAP, -1)
    expert_back = lax.psum(back_part[flat] * keep_rows, "mp")
    logit_grad = (gate_grad * gate * (picked - router)).astype(jnp.bfloat16)
    grad_router = jnp.einsum(
        "td,te->de", normed_two, logit_grad, preferred_element_type=jnp.float32
    )
    second_grad = expert_back + jnp.einsum(
        "te,de->td", logit_grad, w_router, preferred_element_type=jnp.float32
    )
    _, second_pull = jax.vjp(norm_rows, middle, gain_two)
    middle_grad, grad_gain_two = second_pull(second_grad)
    middle_grad = middle_grad + grad_seed
    attn_grad = middle_grad.astype(jnp.bfloat16)
    grad_output_w = jnp.einsum("tc,td->cd", context, attn_grad, preferred_element_type=jnp.float32)
    context_grad = (
        jnp.einsum("td,cd->tc", attn_grad, w_output, preferred_element_type=jnp.float32)
        .astype(jnp.bfloat16)
        .reshape(count, heads, HEAD)
    )
    grad_keys = jnp.zeros((count, heads, HEAD), jnp.float32)
    grad_values = jnp.zeros((count, heads, HEAD), jnp.float32)
    grad_table = jnp.zeros((NB, heads), jnp.float32)
    query_grads = []
    for begin, total in zip(starts, totals):
        scores, onehot, query_block = block_scores()
        probs = jnp.exp(scores - total)
        prob_grad = jnp.einsum(
            "qhd,khd->hqk", context_grad, values, preferred_element_type=jnp.float32
        )
        centre = jnp.sum(probs * prob_grad, axis=-1, keepdims=True)
        score_grad = (probs * (prob_grad - centre)).astype(jnp.bfloat16)
        query_grads.append(
            jnp.einsum("hqk,khd->qhd", score_grad, keys, preferred_element_type=jnp.float32)
        )
        grad_keys = jnp.einsum(
            "hqk,qhd->khd", score_grad, query_block, preferred_element_type=jnp.float32
        )
        grad_values = jnp.einsum(
            "hqk,qhd->khd",
            probs.astype(jnp.bfloat16),
            context_grad,
            preferred_element_type=jnp.float32,
        )
        grad_table = jnp.einsum(
            "hqk,qkb->bh", score_grad, onehot, preferred_element_type=jnp.float32
        )
    query_grad = query_grads[0].reshape(count, inner).astype(jnp.bfloat16)
    key_grad = grad_keys.reshape(count, inner).astype(jnp.bfloat16)
    value_grad = grad_values.reshape(count, inner).astype(jnp.bfloat16)
    grad_query_w = jnp.einsum("td,tc->dc", normed, query_grad, preferred_element_type=jnp.float32)
    grad_key_w = jnp.einsum("td,tc->dc", normed, key_grad, preferred_element_type=jnp.float32)
    grad_value_w = jnp.einsum("td,tc->dc", normed, value_grad, preferred_element_type=jnp.float32)
    first_part = jnp.einsum("tc,dc->td", query_grad, w_query, preferred_element_type=jnp.float32)
    first_part = first_part + jnp.einsum(
        "tc,dc->td", key_grad, w_key, preferred_element_type=jnp.float32
    )
    first_part = first_part + jnp.einsum(
        "tc,dc->td", value_grad, w_value, preferred_element_type=jnp.float32
    )
    first_grad = lax.psum(first_part, "mp")
    _, first_pull = jax.vjp(norm_rows, inputs, gain_one)
    input_grad, grad_gain_one = first_pull(first_grad)
    grad_tokens = middle_grad + input_grad
    table_total = lax.psum(grad_table, "dp")
    gathered = (
        lax.psum_scatter(grad_gain_one, "dp", scatter_dimension=0, tiled=True),
        lax.psum_scatter(grad_query_w, "dp", scatter_dimension=0, tiled=True),
        lax.psum_scatter(grad_key_w, "dp", scatter_dimension=0, tiled=True),
        lax.psum_scatter(grad_value_w, "dp", scatter_dimension=0, tiled=True),
        lax.psum_scatter(grad_output_w, "dp", scatter_dimension=1, tiled=True),
        lax.psum_scatter(grad_gain_two, "dp", scatter_dimension=0, tiled=True),
        lax.psum_scatter(grad_router, "dp", scatter_dimension=0, tiled=True),
        lax.psum_scatter(grad_in_w, "dp", scatter_dimension=1, tiled=True),
        lax.psum_scatter(grad_out_w, "dp", scatter_dimension=2, tiled=True),
    )
    (
        gain_one_sum,
        query_sum,
        key_sum,
        value_sum,
        output_sum,
        gain_two_sum,
        router_sum,
        in_sum,
        out_sum,
    ) = gathered
    return (
        mixed,
        grad_tokens,
        gain_one_sum,
        query_sum,
        key_sum,
        value_sum,
        output_sum,
        table_total,
        gain_two_sum,
        router_sum,
        in_sum,
        out_sum,
    )


def solution(mesh):
    return jax.shard_map(
        shards,
        mesh=mesh,
        in_specs=(
            P("dp", None),
            P(),
            P(None, "mp"),
            P(None, "mp"),
            P(None, "mp"),
            P("mp", None),
            P(None, "mp"),
            P(),
            P(),
            P(None, None, "mp"),
            P(None, "mp", None),
            P("dp", None),
            P("dp", None),
            P("dp"),
        ),
        out_specs=(
            P("dp", None),
            P("dp", None),
            P("dp"),
            P("dp", "mp"),
            P("dp", "mp"),
            P("dp", "mp"),
            P("mp", "dp"),
            P(None, "mp"),
            P("dp"),
            P("dp", None),
            P(None, "dp", "mp"),
            P(None, "mp", "dp"),
        ),
        check_vma=False,
    )
```

profile of v0, /device:TPU:0, one launch (start us, length us, event | category | flops | bytes accessed | tf_op | source)
XLA Modules:
  0.0 1000.1 jit_solution(15323316263035000244)
XLA Ops:
  15.7 5.1 fusion.1
  20.8 4.5 fusion.86
  38.9 47.1 %all-reduce.8.cloned.1.call-done = f32[512,768]{1,0:T(8,128)} async-done(((f32[512,768]{1,0:T(8,128)}), f32[512,768]{1,0:T(8,128)}) %all-reduce.8.cloned.1.call-update) | async-done | bytes 1572880 | tf_op jit(solution)/shard_map/psum | solution.py:122
  94.1 3.4 gather_fusion.2
  97.4 5.4 fusion.42
  102.9 8.4 fusion.76
  111.3 11.6 %fusion.13 = bf16[4,160,1536]{2,1,0:T(8,128)(2,1)} fusion(f32[4,160,1536]{2,1,0:T(8,128)} %copy-done.8, bf16[4,1536,768]{2,1,0:T(8,128)(2,1)} %param.24, bf16[4,160,768]{2,1,0:T(8,128)(2,1)S(1)} %bitcast.93, bf16[4,160]{1,0:T(4,128)(2,1)S(1)} %mul.257), kind=kOutput, calls=%fused_computation.27 | convolution fusion | flops 1530101760 | bytes 16319744 | tf_op jit(solution)/shard_map/ecd,efd->ecf/dot_general | solution.py:140
  123.0 4.7 fusion.89
  130.4 4.9 gather_fusion.1
  135.2 3.3 broadcast_multiply_fusion
  138.8 85.9 %all-reduce.12.cloned.1.call-done = (f32[512,768]{1,0:T(8,128)}, f32[512,768]{1,0:T(8,128)}) async-done(((f32[512,768]{1,0:T(8,128)}, f32[512,768]{1,0:T(8,128)}), (f32[512,768]{1,0:T(8,128)}, f32[512,768]{1,0:T(8,128)})) %all-reduce.12.cloned.1.call-update) | async-done | bytes 3145744 | tf_op jit(solution)/shard_map/psum | solution.py:133
  230.0 3.7 convert_add_fusion.1
  254.8 11.7 %fusion.34 = f32[4,1536,768]{1,2,0:T(8,128)} fusion(bf16[4,160,768]{2,1,0:T(8,128)(2,1)} %bitcast.92, bf16[4,160]{1,0:T(4,128)(2,1)S(1)} %mul.257, f32[4,160,1536]{2,1,0:T(8,128)} %copy-done.8), kind=kOutput, calls=%fused_computation.75 | convolution fusion | flops 1519288320 | bytes 23790848 | tf_op jit(solution)/shard_map/ecf,ecd->efd/dot_general | solution.py:139
  266.6 11.2 %fusion.40 = f32[4,768,1536]{2,1,0:T(8,128)} fusion(bf16[4,160,1536]{2,1,0:T(8,128)(2,1)} %fusion.13, bf16[4,160,768]{2,1,0:T(8,128)(2,1)} %bitcast.91, bf16[4,160]{1,0:T(4,128)(2,1)S(1)} %mul.257), kind=kOutput, calls=%fused_computation.79 | convolution fusion | flops 1510440960 | bytes 21824768 | tf_op jit(solution)/shard_map/ecd,ecf->edf/dot_general | solution.py:143
  279.7 8.1 fusion.30
  287.8 8.8 reduce-scatter.22.cloned.1.call-done
  298.0 52.0 %all-reduce.10.cloned.1.call-done = f32[512,768]{1,0:T(8,128)} async-done(((f32[512,768]{1,0:T(8,128)}), f32[512,768]{1,0:T(8,128)}) %all-reduce.10.cloned.1.call-update) | async-done | bytes 1572880 | tf_op jit(solution)/shard_map/psum | solution.py:205
  352.0 61.4 %all-reduce.2 = (f32[768]{0:T(1024)S(1)}, f32[32,6]{0,1:T(8,128)}, f32[768]{0:T(1024)S(1)}) all-reduce(f32[768]{0:T(1024)S(1)} %get-tuple-element.14, f32[32,6]{0,1:T(8,128)S(1)} %fusion.30, f32[768]{0:T(1024)S(1)} %get-tuple-element.12), channel_id=2, replica_groups=mesh['dp'=16,'mp'=2] {'dp'}, use_global_device_ids=true, to_apply=%region_24.25.clone | all-reduce | flops 1728 | bytes 13824
  414.5 3.0 fusion.20
  417.5 55.8 %reduce-scatter.14.cloned.1.call-done = f32[48,384]{1,0:T(8,128)} async-done(((f32[768,384]{1,0:T(8,128)}), f32[48,384]{1,0:T(8,128)}) %reduce-scatter.14.cloned.1.call-update) | async-done | bytes 73744 | tf_op jit(solution)/shard_map/reduce_scatter | solution.py:214
  473.4 61.1 %reduce-scatter.12.cloned.1.call-done = f32[48,384]{1,0:T(8,128)} async-done(((f32[768,384]{1,0:T(8,128)}), f32[48,384]{1,0:T(8,128)}) %reduce-scatter.12.cloned.1.call-update) | async-done | bytes 73744 | tf_op jit(solution)/shard_map/reduce_scatter | solution.py:213
  534.5 61.3 %reduce-scatter.10.cloned.1.call-done = f32[48,384]{1,0:T(8,128)} async-done(((f32[768,384]{1,0:T(8,128)}), f32[48,384]{1,0:T(8,128)}) %reduce-scatter.10.cloned.1.call-update) | async-done | bytes 73744 | tf_op jit(solution)/shard_map/reduce_scatter | solution.py:212
  595.8 198.6 %reduce-scatter.20.cloned.1.call-done = f32[4,1536,48]{1,2,0:T(8,128)} async-done(((f32[4,1536,768]{1,2,0:T(8,128)}), f32[4,1536,48]{1,2,0:T(8,128)}) %reduce-scatter.20.cloned.1.call-update) | async-done | bytes 1179664 | tf_op jit(solution)/shard_map/reduce_scatter | solution.py:219
  794.4 198.5 %reduce-scatter.18.cloned.1.call-done = f32[4,48,1536]{2,1,0:T(8,128)} async-done(((f32[4,768,1536]{2,1,0:T(8,128)}), f32[4,48,1536]{2,1,0:T(8,128)}) %reduce-scatter.18.cloned.1.call-update) | async-done | bytes 1179664 | tf_op jit(solution)/shard_map/reduce_scatter | solution.py:218
  (163 shorter events, 64.7 us)
Async XLA Ops:
  7.2 22.7 %copy-start = (bf16[384,768]{1,0:T(8,128)(2,1)S(1)}, bf16[384,768]{1,0:T(8,128)(2,1)}, u32[]{:S(2)}) copy-start(bf16[384,768]{1,0:T(8,128)(2,1)} %param.19) | copy-start | bytes 1769476
  7.2 6.1 copy-start.3
  7.2 6.1 copy-start.24
  7.2 78.7 %all-reduce.8.cloned.1.call-start = ((), (), s32[]{:S(2)}) async-start(), calls=%async_computation.7 | async-start | bytes 3145728 | tf_op jit(solution)/shard_map/psum | solution.py:122
  13.3 7.5 copy-start.22
  13.9 6.9 copy-start.20
  14.6 11.7 %copy-start.18 = (bf16[512,384]{0,1:T(8,128)(2,1)}, bf16[512,384]{0,1:T(8,128)(2,1)S(1)}, u32[]{:S(2)}) copy-start(bf16[512,384]{0,1:T(8,128)(2,1)S(1)} %convolution_convert_fusion.7) | copy-start | bytes 1179652
  31.6 193.1 %all-reduce.12.cloned.1.call-start = ((), (), s32[]{:S(2)}) async-start(), calls=%async_computation.16 | async-start | bytes 6291456 | tf_op jit(solution)/shard_map/psum | solution.py:133
  102.9 8.5 copy-start.8
  102.9 8.5 copy-start.12
  102.9 20.1 %slice-start.2 = ((s8[9437184]{0:T(1024)(128)(4,1)}), s8[4194304]{0:T(1024)(128)(4,1)S(1)}, s32[]{:S(2)}) async-start(s8[9437184]{0:T(1024)(128)(4,1)} %bitcast.88), calls=%async_computation.19 | async-start | bytes 8388608
  111.3 11.6 %slice-start.3 = ((s8[9437184]{0:T(1024)(128)(4,1)}), s8[4194304]{0:T(1024)(128)(4,1)S(1)}, s32[]{:S(2)}) async-start(s8[9437184]{0:T(1024)(128)(4,1)} %bitcast.88), calls=%async_computation.20 | async-start | bytes 8388608
  111.3 11.6 %slice-start.4 = ((s8[9437184]{0:T(1024)(128)(4,1)}), s8[1048576]{0:T(1024)(128)(4,1)S(1)}, s32[]{:S(2)}) async-start(s8[9437184]{0:T(1024)(128)(4,1)} %bitcast.88), calls=%async_computation.21 | async-start | bytes 2097152
  138.6 89.1 %copy-start.7 = (f32[512,768]{1,0:T(8,128)S(1)}, f32[512,768]{1,0:T(8,128)}, u32[]{:S(2)}) copy-start(f32[512,768]{1,0:T(8,128)} %copy-done.6) | copy-start | bytes 4718596
  138.6 158.0 %reduce-scatter.22.cloned.1.call-start = ((), (), s32[]{:S(2)}) async-start(), calls=%async_computation.15 | async-start | bytes 417792
  227.7 6.5 slice-start
  240.9 109.1 %all-reduce.10.cloned.1.call-start = ((), (), s32[]{:S(2)}) async-start(), calls=%async_computation.8 | async-start | bytes 3145728 | tf_op jit(solution)/shard_map/psum | solution.py:205
  246.2 171.3 %reduce-scatter.16.cloned.1.call-start = ((), (), s32[]{:S(2)}) async-start(), calls=%async_computation.12 | async-start | bytes 1253376 | tf_op jit(solution)/shard_map/reduce_scatter | solution.py:215
  248.0 225.4 %reduce-scatter.14.cloned.1.call-start = ((), (), s32[]{:S(2)}) async-start(), calls=%async_computation.11 | async-start | bytes 1253376 | tf_op jit(solution)/shard_map/reduce_scatter | solution.py:214
  249.9 284.6 %reduce-scatter.12.cloned.1.call-start = ((), (), s32[]{:S(2)}) async-start(), calls=%async_computation.10 | async-start | bytes 1253376 | tf_op jit(solution)/shard_map/reduce_scatter | solution.py:213
  252.7 343.0 %reduce-scatter.10.cloned.1.call-start = ((), (), s32[]{:S(2)}) async-start(), calls=%async_computation.9 | async-start | bytes 1253376 | tf_op jit(solution)/shard_map/reduce_scatter | solution.py:212
  254.6 539.8 %reduce-scatter.20.cloned.1.call-start = ((), (), s32[]{:S(2)}) async-start(), calls=%async_computation.14 | async-start | bytes 20054016 | tf_op jit(solution)/shard_map/reduce_scatter | solution.py:219
  266.6 726.3 %reduce-scatter.18.cloned.1.call-start = ((), (), s32[]{:S(2)}) async-start(), calls=%async_computation.13 | async-start | bytes 20054016 | tf_op jit(solution)/shard_map/reduce_scatter | solution.py:218
  414.5 578.3 %copy-start.1 = (bf16[384,768]{1,0:T(8,128)(2,1)S(1)}, bf16[384,768]{1,0:T(8,128)(2,1)}, u32[]{:S(2)}) copy-start(bf16[384,768]{1,0:T(8,128)(2,1)} %param.19) | copy-start | bytes 1769476
  (23 other events, 54.5 us)
Sparse Core Ops, SparseCore 0:
  31.7 54.1 all-reduce.7
  138.7 85.9 all-reduce.11
  241.0 55.5 reduce-scatter.21
  299.4 50.5 all-reduce.9
  354.0 58.0 reduce-scatter.15
  416.2 57.1 reduce-scatter.13
  477.6 56.8 reduce-scatter.11
  538.7 57.0 reduce-scatter.9
  600.4 193.8 reduce-scatter.19
  798.9 193.8 reduce-scatter.17
where the time goes:
time: 1010 us; the launch traced here: 1000 us
  waiting for transfers between devices  769 us (76%)
  matrix products  98.4 us (10%)
  blocking collectives  61.4 us (6%)
  local copies, waits for them, and re-layouts  27.5 us (3%)
  other arithmetic  26.9 us (3%)
  between operations  15.9 us (2%)
    reduce_scatter x1, waiting for transfers between devices, shards(): lax.psum_scatter(grad_out_w, 'dp', scatter_dimension=2, tiled=True)  199 us
    reduce_scatter x1, waiting for transfers between devices, shards(): lax.psum_scatter(grad_in_w, 'dp', scatter_dimension=1, tiled=True)  198 us
    psum x1, waiting for transfers between devices, shards(): expert_full = lax.psum(expert_part[flat] * keep_rows, 'mp')  85.9 us
    unnamed x1, blocking collectives  61.4 us
    reduce_scatter x1, waiting for transfers between devices, shards(): lax.psum_scatter(grad_query_w, 'dp', scatter_dimension=0, tiled=True)  61.3 us
    reduce_scatter x1, waiting for transfers between devices, shards(): lax.psum_scatter(grad_key_w, 'dp', scatter_dimension=0, tiled=True)  61.1 us
    reduce_scatter x1, waiting for transfers between devices, shards(): lax.psum_scatter(grad_value_w, 'dp', scatter_dimension=0, tiled=True)  55.8 us
    psum x1, waiting for transfers between devices, shards(): first_grad = lax.psum(first_part, 'mp')  52 us
  transfers between devices with their start and end apart: 10, of which 9 were waited for; matrix products, arithmetic and copies ran while one was open for 6% of the time, Pallas kernels for 0%

commit v1 on v0

v1 whole, which is shorter than its diff:
```python
import jax
import jax.numpy as jnp
from jax import lax
from jax.sharding import PartitionSpec as P

HEAD = 64
NB = 32
E = 4
CAP = 160
CORES = 2
PAIR = 2
LOCAL = E // CORES

EPS = 1e-06
THRESHOLDS = (12, 16, 23, 32, 46, 64, 91)
F32 = jnp.float32
BF16 = jnp.bfloat16


def segments(lengths, count):
    places = jnp.arange(count, dtype=jnp.int32)
    entry = jnp.arange(lengths.shape[0], dtype=jnp.int32)
    ends = jnp.sum(jnp.where(entry[None, :] <= entry[:, None], lengths[None, :], 0), axis=1)
    return jnp.sum((places[:, None] >= ends[None, :]).astype(jnp.int32), axis=1)


def relative_bucket(query_pos, key_pos):
    offset = key_pos[None, :] - query_pos[:, None]
    distance = jnp.abs(offset)
    far_side = 8 + sum(((distance >= edge).astype(jnp.int32) for edge in THRESHOLDS))
    near = jnp.where(distance < 8, distance, far_side)
    return jnp.where(offset > 0, NB // 2, 0) + near


def ranks(expert_ids):
    place = jnp.arange(expert_ids.shape[0], dtype=jnp.int32)
    earlier = (expert_ids[:, None] == expert_ids[None, :]) & (place[None, :] < place[:, None])
    return jnp.sum(earlier.astype(jnp.int32), axis=1)


def norm_rows(values, gain):
    return values * lax.rsqrt(jnp.mean(values * values, axis=-1, keepdims=True) + EPS) * gain


def mm(spec, left, right, precision=None):
    return jnp.einsum(spec, left, right, preferred_element_type=F32, precision=precision)


def solution(mesh):
    n_dp, n_mp = mesh.shape["dp"], mesh.shape["mp"]
    line = n_dp // (CORES * PAIR)

    def swap(value, stride):
        return lax.ppermute(value, "dp", [(i, i ^ stride) for i in range(n_dp)])

    def mp_other(value):
        return lax.ppermute(value, "mp", [(0, 1), (1, 0)])

    def mp_sum(value):
        return value + mp_other(value) if n_mp == 2 else lax.psum(value, "mp")

    def dp_sum(value):
        if n_dp & (n_dp - 1):
            return lax.psum(value, "dp")
        stride = 1
        while stride < n_dp:
            value = value + swap(value, stride)
            stride *= 2
        return value

    def shards(
        tokens,
        gain_attn,
        w_query,
        w_key,
        w_value,
        w_output,
        position_table,
        gain_moe,
        w_router,
        w_in,
        w_out,
        cotangent,
        seq_lengths,
        expert_ids,
    ):
        device = lax.axis_index("dp")
        core = device % CORES
        side = (device // CORES) % PAIR
        row = device // (CORES * PAIR)
        count, width = tokens.shape
        share = width // n_dp
        heads = position_table.shape[1]
        inner = heads * HEAD

        def pick(value, index, axis):
            return lax.dynamic_index_in_dim(value, index, axis, keepdims=False)

        def flow(own, up):
            got = None
            for step in range(1, line):
                if up:
                    index = jnp.minimum(line - step + row, line - 1)
                    hops = [(i, i + 1) for i in range(step)]
                else:
                    index = jnp.maximum(step - line + row, 0)
                    hops = [(line - 1 - i, line - 2 - i) for i in range(step)]
                piece = pick(own, index, 0)
                if got is not None:
                    piece = piece + got
                block = CORES * PAIR
                got = lax.ppermute(
                    piece, "dp", [(a * block + k, b * block + k) for a, b in hops for k in range(block)]
                )
            return got

        def line_sum(own):
            if line == 1:
                return own[0]
            if line > 4:
                block = CORES * PAIR
                groups = [[r * block + k for r in range(line)] for k in range(block)]
                return lax.psum_scatter(own, "dp", scatter_dimension=0, axis_index_groups=groups)
            return pick(own, row, 0) + flow(own, True) + flow(own, False)

        def chip_sum(own):
            got = swap(pick(own, 1 - side, 1), CORES)
            return line_sum(pick(own, side, 1) + got)

        def expert_sum(grad):
            own = chip_sum(grad.reshape(line, PAIR, CORES * share, -1)).reshape(CORES, share, -1)
            return pick(own, core, 0), swap(pick(own, 1 - core, 0), 1)

        def dense_sum(grad):
            own = grad.reshape(line, PAIR, CORES, share, -1)
            got = swap(pick(own, 1 - core, 2), 1)
            return chip_sum(pick(own, core, 2) + got)

        segment = segments(seq_lengths[0], count)
        place = jnp.arange(count, dtype=jnp.int32)
        inputs = tokens.astype(F32)
        gain_one = gain_attn.astype(F32)
        gain_two = gain_moe.astype(F32)
        bucket_ids = jnp.arange(NB, dtype=jnp.int32)
        normed = norm_rows(inputs, gain_one).astype(BF16)
        query = mm("td,dc->tc", normed, w_query).astype(BF16).reshape(count, heads, HEAD)
        keys = mm("td,dc->tc", normed, w_key).astype(BF16).reshape(count, heads, HEAD)
        values = mm("td,dc->tc", normed, w_value).astype(BF16).reshape(count, heads, HEAD)

        bucket = relative_bucket(place, place)
        onehot = (bucket[:, :, None] == bucket_ids[None, None, :]).astype(BF16)
        allowed = segment[:, None] == segment[None, :]

        def all_scores():
            bias = mm("qkb,bh->hqk", onehot, position_table)
            scores = mm("qhd,khd->hqk", query, keys) + bias
            return jnp.where(allowed[None], scores, -1000000000.0)

        scores = all_scores()
        peak = jnp.max(scores, axis=-1, keepdims=True)
        total = peak + jnp.log(jnp.sum(jnp.exp(scores - peak), axis=-1, keepdims=True))
        probs = jnp.exp(scores - total).astype(BF16)
        context = mm("hqk,khd->qhd", probs, values).reshape(count, inner).astype(BF16)
        middle = inputs + mp_sum(mm("tc,cd->td", context, w_output))

        rank = ranks(expert_ids)
        local = (expert_ids - LOCAL * core) % E
        slot = jnp.where(rank < CAP, local * CAP + rank, -1)
        select = jnp.arange(E * CAP, dtype=jnp.int32)[:, None] == slot[None, :]
        select_low = select.astype(BF16)
        select_full = select.astype(F32)
        picked = (expert_ids[:, None] == jnp.arange(E, dtype=jnp.int32)[None, :]).astype(F32)
        my_in = lax.dynamic_slice_in_dim(w_in, LOCAL * core, LOCAL, 0)
        my_out = lax.dynamic_slice_in_dim(w_out, LOCAL * core, LOCAL, 0)

        half = LOCAL * CAP

        def to_experts(rows):
            slots = mm("st,td->sd", select_low, rows)
            return slots[:half], swap(slots[half:], 1)

        def scaled(parts, weight):
            both = [
                (part * scale[:, None]).reshape(LOCAL, CAP, width)
                for part, scale in zip(parts, weight)
            ]
            return jnp.concatenate(both, axis=1).astype(BF16)

        def slot_values(values):
            slots = jnp.sum(jnp.where(select, values[None, :], 0.0), axis=1)
            return slots[:half], swap(slots[half:], 1)

        live = slot_values(jnp.ones((count,), F32))
        seed_slots = to_experts(cotangent)

        def to_tokens(slots):
            got = swap(slots[:, CAP:], 1)
            both = jnp.concatenate([slots[:, :CAP], got], axis=0).reshape(E * CAP, width)
            return mm("st,sd->td", select_full, both, lax.Precision.HIGH)

        normed_two = norm_rows(middle, gain_two).astype(BF16)
        dispatch = scaled(to_experts(normed_two), live)
        logits = mm("td,de->te", normed_two, w_router)
        router = jax.nn.softmax(logits, axis=-1)
        gate = jnp.sum(router * picked, axis=1, keepdims=True)
        grad_seed = cotangent.astype(F32)
        slot_grad = scaled(seed_slots, slot_values(gate[:, 0]))

        pre_act = mm("ecd,edf->ecf", dispatch, my_in)
        hidden, gelu_pull = jax.vjp(jax.nn.gelu, pre_act)
        hidden = hidden.astype(BF16)
        grad_out_rows = mm("ecd,ecf->edf", slot_grad, hidden)
        out_sums = [expert_sum(grad_out_rows[k]) for k in range(LOCAL)]
        hidden_grad = mm("ecd,efd->ecf", slot_grad, my_out)
        pre_grad = gelu_pull(hidden_grad)[0].astype(BF16)
        grad_in_rows = mm("ecd,ecf->edf", dispatch, pre_grad)
        in_sums = [expert_sum(grad_in_rows[k]) for k in range(LOCAL)]
        expert_part = to_tokens(mm("ecf,efd->ecd", hidden, my_out))
        back_part = to_tokens(mm("ecf,edf->ecd", pre_grad, my_in))
        gate_grad = mp_sum(jnp.sum(grad_seed * expert_part, axis=1, keepdims=True))
        expert_back = mp_sum(back_part)
        mixed = (middle + gate * mp_sum(expert_part)).astype(BF16)

        logit_grad = (gate_grad * gate * (picked - router)).astype(BF16)
        grad_router = mm("td,te->de", normed_two, logit_grad)
        second_grad = expert_back + mm("te,de->td", logit_grad, w_router)
        _, second_pull = jax.vjp(norm_rows, middle, gain_two)
        middle_grad, grad_gain_two = second_pull(second_grad)
        middle_grad = middle_grad + grad_seed
        attn_grad = middle_grad.astype(BF16)
        grad_output_rows = mm("td,tc->dc", attn_grad, context)
        context_grad = (
            mm("td,cd->tc", attn_grad, w_output).astype(BF16).reshape(count, heads, HEAD)
        )
        probs = jnp.exp(all_scores() - total)
        prob_grad = mm("qhd,khd->hqk", context_grad, values)
        centre = jnp.sum(probs * prob_grad, axis=-1, keepdims=True)
        score_grad = (probs * (prob_grad - centre)).astype(BF16)
        query_grad = mm("hqk,khd->qhd", score_grad, keys).reshape(count, inner).astype(BF16)
        key_grad = mm("hqk,qhd->khd", score_grad, query).reshape(count, inner).astype(BF16)
        value_grad = (
            mm("hqk,qhd->khd", probs.astype(BF16), context_grad).reshape(count, inner).astype(BF16)
        )
        grad_table = mm("hqk,qkb->bh", score_grad, onehot)
        first_part = (
            mm("tc,dc->td", query_grad, w_query)
            + mm("tc,dc->td", key_grad, w_key)
            + mm("tc,dc->td", value_grad, w_value)
        )
        first_grad = mp_sum(first_part)
        grad_query_rows = mm("td,tc->dc", normed, query_grad)
        grad_key_rows = mm("td,tc->dc", normed, key_grad)
        grad_value_rows = mm("td,tc->dc", normed, value_grad)
        dense = dense_sum(
            jnp.concatenate(
                [grad_query_rows, grad_key_rows, grad_value_rows, grad_output_rows], axis=1
            )
        )
        _, first_pull = jax.vjp(norm_rows, inputs, gain_one)
        input_grad, _ = first_pull(first_grad)
        grad_tokens = middle_grad + input_grad
        grad_gain_one = mp_sum(first_pull(first_part)[1])
        small = jnp.concatenate(
            [
                grad_gain_one[None],
                grad_gain_two[None],
                grad_router.T,
                jnp.pad(grad_table.T, ((0, 0), (0, width - NB))),
            ],
            axis=0,
        )
        small = dp_sum(small)
        table_total = small[2 + E :, :NB].T
        small = lax.dynamic_slice_in_dim(small[: 2 + E], device * share, share, 1)

        def by_expert(sums):
            mine = jnp.stack([own for own, _ in sums])
            other = jnp.stack([got for _, got in sums])
            first = core == 0
            return jnp.concatenate(
                [jnp.where(first, mine, other), jnp.where(first, other, mine)], axis=0
            )

        return (
            mixed,
            grad_tokens,
            small[0],
            dense[:, :inner],
            dense[:, inner : 2 * inner],
            dense[:, 2 * inner : 3 * inner],
            dense[:, 3 * inner :].T,
            table_total,
            small[1],
            small[2:].T,
            by_expert(in_sums),
            jnp.swapaxes(by_expert(out_sums), 1, 2),
        )

    return jax.shard_map(
        shards,
        mesh=mesh,
        in_specs=(
            P("dp", None),
            P(),
            P(None, "mp"),
            P(None, "mp"),
            P(None, "mp"),
            P("mp", None),
            P(None, "mp"),
            P(),
            P(),
            P(None, None, "mp"),
            P(None, "mp", None),
            P("dp", None),
            P("dp", None),
            P("dp"),
        ),
        out_specs=(
            P("dp", None),
            P("dp", None),
            P("dp"),
            P("dp", "mp"),
            P("dp", "mp"),
            P("dp", "mp"),
            P("mp", "dp"),
            P(None, "mp"),
            P("dp"),
            P("dp", None),
            P(None, "dp", "mp"),
            P(None, "mp", "dp"),
        ),
        check_vma=False,
    )
```

time: 1010 us -> 588 us (0.58)
  waiting for transfers between devices: 769 us -> 313 us
  starting transfers between devices: 0.8 us -> 114 us
  blocking collectives: 61.4 us -> 0 us
  matrix products: 98.4 us -> 71 us
  local copies, waits for them, and re-layouts: 27.5 us -> 42.1 us
  between operations: 15.9 us -> 2.39 us
  other arithmetic: 26.9 us -> 38.2 us
    reduce_scatter x6 -> x0, waiting for transfers between devices: 575 us -> none  [the longest x1 199 us: shards(): lax.psum_scatter(grad_out_w, 'dp', scatter_dimension=2, tiled=True)]
    ppermute x0 -> x56, waiting for transfers between devices: none -> 313 us  [the longest x20 189 us: swap(): return lax.ppermute(value, 'dp', [(i, i ^ stride) for i in range(n_dp)])]
    psum x3 -> x0, waiting for transfers between devices: 185 us -> none  [the longest x1 85.9 us: shards(): expert_full = lax.psum(expert_part[flat] * keep_rows, 'mp')]
    ppermute x0 -> x56, starting transfers between devices: none -> 114 us  [the longest x30 88.8 us: flow(): lax.ppermute(piece, 'dp', [(a * block + k, b * block + k) for a, b in hop...]
    unnamed x1 -> x0, blocking collectives: 61.4 us -> none
    dot_general x28 -> x33, matrix products: 97.2 us -> 71 us  [mm(): jnp.einsum(spec, left, right, preferred_element_type=F32, precision=preci...]
    squeeze x0 -> x12, local copies, waits for them, and re-layouts: none -> 14.1 us  [the longest x11 13.6 us: pick(): return lax.dynamic_index_in_dim(value, index, axis, keepdims=False)]
    gather x4 -> x0, local copies, waits for them, and re-layouts: 13.8 us -> none  [the longest x1 4.86 us: shards(): expert_full = lax.psum(expert_part[flat] * keep_rows, 'mp')]
  transfers between devices with their start and end apart: 10 -> 56, of which waited for: 9 -> 25; matrix products, arithmetic and copies ran while one was open for 6% -> 18% of each run, Pallas kernels for 0% -> 0%
where the time goes in v1:
time: 588 us; the launch traced here: 581 us
  waiting for transfers between devices  313 us (53%)
  starting transfers between devices  114 us (19%)
  matrix products  71 us (12%)
  local copies, waits for them, and re-layouts  42.1 us (7%)
  other arithmetic  38.2 us (6%)
    ppermute x20, waiting for transfers between devices, swap(): return lax.ppermute(value, 'dp', [(i, i ^ stride) for i in range(n_dp)])  189 us
    ppermute x30, starting transfers between devices, flow(): lax.ppermute(piece, 'dp', [(a * block + k, b * block + k) for a, b in hop...  88.8 us
    ppermute x30, waiting for transfers between devices, flow(): lax.ppermute(piece, 'dp', [(a * block + k, b * block + k) for a, b in hop...  88.5 us
    dot_general x33, matrix products, mm(): jnp.einsum(spec, left, right, preferred_element_type=F32, precision=preci...  71 us
    ppermute x6, waiting for transfers between devices, mp_other(): return lax.ppermute(value, 'mp', [(0, 1), (1, 0)])  36.3 us
    ppermute x20, starting transfers between devices, swap(): return lax.ppermute(value, 'dp', [(i, i ^ stride) for i in range(n_dp)])  15.2 us
    squeeze x11, local copies, waits for them, and re-layouts, pick(): return lax.dynamic_index_in_dim(value, index, axis, keepdims=False)  13.6 us
  transfers between devices with their start and end apart: 56, of which 25 were waited for; matrix products, arithmetic and copies ran while one was open for 18% of the time, Pallas kernels for 0%

profile of v1, /device:TPU:0, one launch (start us, length us, event | category | flops | bytes accessed | tf_op | source)
XLA Modules:
  0.0 581.2 jit_solution(9700013944538409653)
XLA Ops:
  7.0 5.1 fusion.1
  25.2 34.2 %collective-permute-done = f32[512,768]{1,0:T(8,128)} collective-permute-done((f32[512,768]{1,0:T(8,128)S(1)}, f32[512,768]{1,0:T(8,128)}, u32[]{:S(2)}, u32[]{:S(2)}) %collective-permute-start) | collective-permute-done | bytes 1572896 | tf_op jit(solution)/shard_map/ppermute | solution.py:57
  84.0 5.6 fusion.59
  95.5 6.8 %fusion.104 = (f32[1,768,1536]{2,1,0:T(8,128)S(1)}, f32[1,768,1536]{2,1,0:T(8,128)}) fusion(f32[2,768,1536]{2,1,0:T(8,128)} %fusion.59), kind=kLoop, calls=%fused_computation.227 | loop fusion | bytes 18874368 | tf_op jit(solution)/shard_map/slice | solution.py:217
  127.4 34.2 %collective-permute-done.31 = f32[4,96,1536]{2,1,0:T(8,128)} collective-permute-done((f32[4,96,1536]{2,1,0:T(8,128)}, f32[4,96,1536]{2,1,0:T(8,128)}, u32[]{:S(2)}, u32[]{:S(2)}) %collective-permute-start.31) | collective-permute-done | bytes 2359328 | tf_op jit(solution)/shard_map/ppermute | solution.py:54
  166.5 45.6 %collective-permute-done.24 = f32[4,96,1536]{2,1,0:T(8,128)} collective-permute-done((f32[4,96,1536]{2,1,0:T(8,128)}, f32[4,96,1536]{2,1,0:T(8,128)}, u32[]{:S(2)}, u32[]{:S(2)}) %collective-permute-start.24) | collective-permute-done | bytes 2359328 | tf_op jit(solution)/shard_map/ppermute | solution.py:54
  220.1 42.5 %collective-permute-done.47 = f32[4,96,1536]{2,1,0:T(8,128)S(1)} collective-permute-done((f32[4,96,1536]{2,1,0:T(8,128)S(1)}, f32[4,96,1536]{2,1,0:T(8,128)S(1)}, u32[]{:S(2)}, u32[]{:S(2)}) %collective-permute-start.47) | collective-permute-done | bytes 2359328 | tf_op jit(solution)/shard_map/ppermute | solution.py:54
  265.7 46.9 %collective-permute-done.40 = f32[4,96,1536]{2,1,0:T(8,128)S(1)} collective-permute-done((f32[4,96,1536]{2,1,0:T(8,128)S(1)}, f32[4,96,1536]{2,1,0:T(8,128)S(1)}, u32[]{:S(2)}, u32[]{:S(2)}) %collective-permute-start.40) | collective-permute-done | bytes 2359328 | tf_op jit(solution)/shard_map/ppermute | solution.py:54
  338.9 9.6 %fusion.36 = f32[6,32]{1,0:T(8,128)S(1)} fusion(s32[512,512]{0,1:T(8,128)} %copy-done.15, bf16[6,512,512]{1,2,0:T(8,128)(2,1)} %copy-done.3), kind=kOutput, calls=%fused_computation.89 | convolution fusion | flops 109051904 | bytes 4195072 | tf_op jit(solution)/shard_map/hqk,qkb->bh/dot_general | solution.py:46
  357.6 6.1 %copy.49 = f32[768,1536]{1,0:T(8,128)} copy(f32[768,1536]{0,1:T(8,128)} %pad_maximum_fusion) | data formatting | bytes 9437184 | tf_op jit(solution)/shard_map/concatenate | solution.py:255
  375.9 10.0 %collective-permute-done.41 = f32[96,1536]{1,0:T(8,128)S(1)} collective-permute-done((f32[96,1536]{1,0:T(8,128)S(1)}, f32[96,1536]{1,0:T(8,128)S(1)}, u32[]{:S(2)}, u32[]{:S(2)}) %collective-permute-start.41) | collective-permute-done | bytes 589856 | tf_op jit(solution)/shard_map/ppermute | solution.py:112
  391.2 7.4 %collective-permute-done.33 = f32[96,1536]{1,0:T(8,128)S(1)} collective-permute-done((f32[96,1536]{1,0:T(8,128)S(1)}, f32[96,1536]{1,0:T(8,128)S(1)}, u32[]{:S(2)}, u32[]{:S(2)}) %collective-permute-start.33) | collective-permute-done | bytes 589856 | tf_op jit(solution)/shard_map/ppermute | solution.py:112
  405.8 5.4 collective-permute-done.26
  417.0 6.9 %collective-permute-done.49 = f32[96,1536]{1,0:T(8,128)S(1)} collective-permute-done((f32[96,1536]{1,0:T(8,128)S(1)}, f32[96,1536]{1,0:T(8,128)S(1)}, u32[]{:S(2)}, u32[]{:S(2)}) %collective-permute-start.49) | collective-permute-done | bytes 589856 | tf_op jit(solution)/shard_map/ppermute | solution.py:112
  424.7 5.0 collective-permute-start.34
  429.8 6.8 %collective-permute-done.42 = f32[96,1536]{1,0:T(8,128)S(1)} collective-permute-done((f32[96,1536]{1,0:T(8,128)S(1)}, f32[96,1536]{1,0:T(8,128)S(1)}, u32[]{:S(2)}, u32[]{:S(2)}) %collective-permute-start.42) | collective-permute-done | bytes 589856 | tf_op jit(solution)/shard_map/ppermute | solution.py:112
  449.7 23.3 %collective-permute-start.50 = (f32[96,1536]{1,0:T(8,128)S(1)}, f32[96,1536]{1,0:T(8,128)S(1)}, u32[]{:S(2)}, u32[]{:S(2)}) collective-permute-start(f32[96,1536]{1,0:T(8,128)S(1)} %get-tuple-element.28), channel_id=1, source_target_pairs={{0,8},{2,10},{4,12},{6,14},{8,16},{10,18},{12,20},{14,22},{16,24},... | collective-permute-start | bytes 1769480 | tf_op jit(solution)/shard_map/ppermute | solution.py:112
  477.2 5.5 collective-permute-start.14
  501.4 15.1 %collective-permute-done.37 = f32[96,1536]{1,0:T(8,128)S(1)} collective-permute-done((f32[96,1536]{1,0:T(8,128)S(1)}, f32[96,1536]{1,0:T(8,128)S(1)}, u32[]{:S(2)}, u32[]{:S(2)}) %collective-permute-start.37) | collective-permute-done | bytes 589856 | tf_op jit(solution)/shard_map/ppermute | solution.py:112
  519.5 9.7 %collective-permute-done.30 = f32[96,1536]{1,0:T(8,128)S(1)} collective-permute-done((f32[96,1536]{1,0:T(8,128)S(1)}, f32[96,1536]{1,0:T(8,128)S(1)}, u32[]{:S(2)}, u32[]{:S(2)}) %collective-permute-start.30) | collective-permute-done | bytes 589856 | tf_op jit(solution)/shard_map/ppermute | solution.py:112
  530.6 7.4 %collective-permute-done.17 = f32[4,48,1536]{2,1,0:T(8,128)S(1)} collective-permute-done((f32[4,48,1536]{2,1,0:T(8,128)S(1)}, f32[4,48,1536]{2,1,0:T(8,128)S(1)}, u32[]{:S(2)}, u32[]{:S(2)}) %collective-permute-start.17) | collective-permute-done | bytes 1179680 | tf_op jit(solution)/shard_map/ppermute | solution.py:54
  553.6 6.3 %collective-permute-done.19 = f32[48,1536]{1,0:T(8,128)S(1)} collective-permute-done((f32[48,1536]{1,0:T(8,128)S(1)}, f32[48,1536]{1,0:T(8,128)S(1)}, u32[]{:S(2)}, u32[]{:S(2)}) %collective-permute-start.19) | collective-permute-done | bytes 294944 | tf_op jit(solution)/shard_map/ppermute | solution.py:112
  560.9 5.0 collective-permute-start.20
  571.7 8.5 %collective-permute-done.23 = f32[48,1536]{1,0:T(8,128)S(1)} collective-permute-done((f32[48,1536]{1,0:T(8,128)S(1)}, f32[48,1536]{1,0:T(8,128)S(1)}, u32[]{:S(2)}, u32[]{:S(2)}) %collective-permute-start.23) | collective-permute-done | bytes 294944 | tf_op jit(solution)/shard_map/ppermute | solution.py:112
  (333 shorter events, 220.0 us)
Async XLA Ops:
  21.9 37.5 %collective-permute-start = (f32[512,768]{1,0:T(8,128)S(1)}, f32[512,768]{1,0:T(8,128)}, u32[]{:S(2)}, u32[]{:S(2)}) collective-permute-start(f32[512,768]{1,0:T(8,128)S(1)} %fusion.111), channel_id=1, source_target_pairs={{0,1},{1,0},{2,3},{3,2},{4,5},{5,4},{6,7},{7,6},{8,9},{9,8},{10,11... | collective-permute-start | bytes 4718600 | tf_op jit(solution)/shard_map/ppermute | solution.py:57
  95.3 26.6 %collective-permute-start.7 = (f32[2,160,768]{2,1,0:T(8,128)}, f32[2,160,768]{2,1,0:T(8,128)}, u32[]{:S(2)}, u32[]{:S(2)}) collective-permute-start(f32[2,160,768]{2,1,0:T(8,128)} %get-tuple-element.41), channel_id=1, source_target_pairs={{0,2},{2,0},{4,6},{6,4},{8,10},{10,8},{12,14},{14,12},{16,18},{18,... | collective-permute-start | bytes 2949128 | tf_op jit(solution)/shard_map/ppermute | solution.py:54
  107.2 54.4 %collective-permute-start.31 = (f32[4,96,1536]{2,1,0:T(8,128)}, f32[4,96,1536]{2,1,0:T(8,128)}, u32[]{:S(2)}, u32[]{:S(2)}) collective-permute-start(f32[4,96,1536]{2,1,0:T(8,128)} %dynamic-slice_bitcast_fusion.2), channel_id=1, source_target_pairs={{0,4},{2,6},{4,0},{6,2},{8,12},{10,14},{12,8},{14,10},{16,20},{18,... | collective-permute-start | bytes 7077896 | tf_op jit(solution)/shard_map/ppermute | solution.py:54
  110.5 101.6 %collective-permute-start.24 = (f32[4,96,1536]{2,1,0:T(8,128)}, f32[4,96,1536]{2,1,0:T(8,128)}, u32[]{:S(2)}, u32[]{:S(2)}) collective-permute-start(f32[4,96,1536]{2,1,0:T(8,128)} %dynamic-slice_bitcast_fusion.3), channel_id=1, source_target_pairs={{0,4},{2,6},{4,0},{6,2},{8,12},{10,14},{12,8},{14,10},{16,20},{18,... | collective-permute-start | bytes 7077896 | tf_op jit(solution)/shard_map/ppermute | solution.py:54
  115.7 146.9 %collective-permute-start.47 = (f32[4,96,1536]{2,1,0:T(8,128)S(1)}, f32[4,96,1536]{2,1,0:T(8,128)S(1)}, u32[]{:S(2)}, u32[]{:S(2)}) collective-permute-start(f32[4,96,1536]{2,1,0:T(8,128)S(1)} %dynamic-slice_bitcast_fusion), channel_id=1, source_target_pairs={{0,4},{2,6},{4,0},{6,2},{8,12},{10,14},{12,8},{14,10},{16,20},{18,... | collective-permute-start | bytes 7077896 | tf_op jit(solution)/shard_map/ppermute | solution.py:54
  117.7 194.9 %collective-permute-start.40 = (f32[4,96,1536]{2,1,0:T(8,128)S(1)}, f32[4,96,1536]{2,1,0:T(8,128)S(1)}, u32[]{:S(2)}, u32[]{:S(2)}) collective-permute-start(f32[4,96,1536]{2,1,0:T(8,128)S(1)} %dynamic-slice_bitcast_fusion.1), channel_id=1, source_target_pairs={{0,4},{2,6},{4,0},{6,2},{8,12},{10,14},{12,8},{14,10},{16,20},{18,... | collective-permute-start | bytes 7077896 | tf_op jit(solution)/shard_map/ppermute | solution.py:54
  126.6 192.2 %collective-permute-start.8 = (f32[512,768]{1,0:T(8,128)S(1)}, f32[512,768]{1,0:T(8,128)S(1)}, u32[]{:S(2)}, u32[]{:S(2)}) collective-permute-start(f32[512,768]{1,0:T(8,128)S(1)} %fusion.32), channel_id=1, source_target_pairs={{0,1},{1,0},{2,3},{3,2},{4,5},{5,4},{6,7},{7,6},{8,9},{9,8},{10,11... | collective-permute-start | bytes 4718600 | tf_op jit(solution)/shard_map/ppermute | solution.py:57
  161.6 159.5 %collective-permute-start.4 = (f32[512,768]{1,0:T(8,128)S(1)}, f32[512,768]{1,0:T(8,128)S(1)}, u32[]{:S(2)}, u32[]{:S(2)}) collective-permute-start(f32[512,768]{1,0:T(8,128)S(1)} %get-tuple-element.81), channel_id=1, source_target_pairs={{0,1},{1,0},{2,3},{3,2},{4,5},{5,4},{6,7},{7,6},{8,9},{9,8},{10,11... | collective-permute-start | bytes 4718600 | tf_op jit(solution)/shard_map/ppermute | solution.py:57
  212.1 155.2 %collective-permute-start.32 = (f32[96,1536]{1,0:T(8,128)}, f32[96,1536]{1,0:T(8,128)}, u32[]{:S(2)}, u32[]{:S(2)}) collective-permute-start(f32[96,1536]{1,0:T(8,128)} %get-tuple-element.38), channel_id=1, source_target_pairs={{0,8},{2,10},{4,12},{6,14},{1,9},{3,11},{5,13},{7,15}} | collective-permute-start | bytes 1769480 | tf_op jit(solution)/shard_map/ppermute | solution.py:112
  262.6 127.9 %collective-permute-start.35 = (f32[96,1536]{1,0:T(8,128)}, f32[96,1536]{1,0:T(8,128)}, u32[]{:S(2)}, u32[]{:S(2)}) collective-permute-start(f32[96,1536]{1,0:T(8,128)} %get-tuple-element.39), channel_id=1, source_target_pairs={{24,16},{26,18},{28,20},{30,22},{25,17},{27,19},{29,21},{31,23}} | collective-permute-start | bytes 1769480 | tf_op jit(solution)/shard_map/ppermute | solution.py:112
  312.6 58.2 %collective-permute-start.25 = (f32[96,1536]{1,0:T(8,128)}, f32[96,1536]{1,0:T(8,128)}, u32[]{:S(2)}, u32[]{:S(2)}) collective-permute-start(f32[96,1536]{1,0:T(8,128)} %get-tuple-element.34), channel_id=1, source_target_pairs={{0,8},{2,10},{4,12},{6,14},{1,9},{3,11},{5,13},{7,15}} | collective-permute-start | bytes 1769480 | tf_op jit(solution)/shard_map/ppermute | solution.py:112
  318.7 85.5 %collective-permute-start.28 = (f32[96,1536]{1,0:T(8,128)}, f32[96,1536]{1,0:T(8,128)}, u32[]{:S(2)}, u32[]{:S(2)}) collective-permute-start(f32[96,1536]{1,0:T(8,128)} %get-tuple-element.35), channel_id=1, source_target_pairs={{24,16},{26,18},{28,20},{30,22},{25,17},{27,19},{29,21},{31,23}} | collective-permute-start | bytes 1769480 | tf_op jit(solution)/shard_map/ppermute | solution.py:112
  322.3 51.1 %collective-permute-start.48 = (f32[96,1536]{1,0:T(8,128)}, f32[96,1536]{1,0:T(8,128)}, u32[]{:S(2)}, u32[]{:S(2)}) collective-permute-start(f32[96,1536]{1,0:T(8,128)} %get-tuple-element.30), channel_id=1, source_target_pairs={{0,8},{2,10},{4,12},{6,14},{1,9},{3,11},{5,13},{7,15}} | collective-permute-start | bytes 1769480 | tf_op jit(solution)/shard_map/ppermute | solution.py:112
  367.4 49.5 %collective-permute-start.51 = (f32[96,1536]{1,0:T(8,128)S(1)}, f32[96,1536]{1,0:T(8,128)S(1)}, u32[]{:S(2)}, u32[]{:S(2)}) collective-permute-start(f32[96,1536]{1,0:T(8,128)S(1)} %copy-done.37), channel_id=1, source_target_pairs={{24,16},{26,18},{28,20},{30,22},{25,17},{27,19},{29,21},{31,23}} | collective-permute-start | bytes 1769480 | tf_op jit(solution)/shard_map/ppermute | solution.py:112
  386.0 25.3 %collective-permute-start.26 = (f32[96,1536]{1,0:T(8,128)S(1)}, f32[96,1536]{1,0:T(8,128)S(1)}, u32[]{:S(2)}, u32[]{:S(2)}) collective-permute-start(f32[96,1536]{1,0:T(8,128)S(1)} %bitcast_add_fusion.24), channel_id=1, source_target_pairs={{0,8},{2,10},{4,12},{6,14},{8,16},{10,18},{12,20},{14,22},{1,9},{3... | collective-permute-start | bytes 1769480 | tf_op jit(solution)/shard_map/ppermute | solution.py:112
  390.5 34.2 %collective-permute-start.44 = (f32[96,1536]{1,0:T(8,128)S(1)}, f32[96,1536]{1,0:T(8,128)S(1)}, u32[]{:S(2)}, u32[]{:S(2)}) collective-permute-start(f32[96,1536]{1,0:T(8,128)S(1)} %copy-done.36), channel_id=1, source_target_pairs={{24,16},{26,18},{28,20},{30,22},{25,17},{27,19},{29,21},{31,23}} | collective-permute-start | bytes 1769480 | tf_op jit(solution)/shard_map/ppermute | solution.py:112
  404.3 33.2 %collective-permute-start.10 = (f32[512,768]{1,0:T(8,128)S(1)}, f32[512,768]{1,0:T(8,128)S(1)}, u32[]{:S(2)}, u32[]{:S(2)}) collective-permute-start(f32[512,768]{1,0:T(8,128)S(1)} %add_add_fusion.2), channel_id=1, source_target_pairs={{0,1},{1,0},{2,3},{3,2},{4,5},{5,4},{6,7},{7,6},{8,9},{9,8},{10,11... | collective-permute-start | bytes 4718600 | tf_op jit(solution)/shard_map/ppermute | solution.py:57
  416.9 81.5 %collective-permute-start.16 = (f32[4,2,48,1536]{3,2,1,0:T(8,128)S(1)}, f32[4,2,48,1536]{3,2,1,0:T(8,128)S(1)}, u32[]{:S(2)}, u32[]{:S(2)}) collective-permute-start(f32[4,2,48,1536]{3,2,1,0:T(8,128)S(1)} %dynamic-slice_bitcast_fusion.4), channel_id=1, source_target_pairs={{0,2},{2,0},{4,6},{6,4},{8,10},{10,8},{12,14},{14,12},{16,18},{18,... | collective-permute-start | bytes 7077896 | tf_op jit(solution)/shard_map/ppermute | solution.py:54
  424.7 75.4 %collective-permute-start.34 = (f32[96,1536]{1,0:T(8,128)S(1)}, f32[96,1536]{1,0:T(8,128)S(1)}, u32[]{:S(2)}, u32[]{:S(2)}) collective-permute-start(f32[96,1536]{1,0:T(8,128)S(1)} %get-tuple-element.36), channel_id=1, source_target_pairs={{0,8},{2,10},{4,12},{6,14},{8,16},{10,18},{12,20},{14,22},{16,24},... | collective-permute-start | bytes 1769480 | tf_op jit(solution)/shard_map/ppermute | solution.py:112
  437.5 80.7 %collective-permute-start.27 = (f32[96,1536]{1,0:T(8,128)S(1)}, f32[96,1536]{1,0:T(8,128)S(1)}, u32[]{:S(2)}, u32[]{:S(2)}) collective-permute-start(f32[96,1536]{1,0:T(8,128)S(1)} %get-tuple-element.32), channel_id=1, source_target_pairs={{0,8},{2,10},{4,12},{6,14},{8,16},{10,18},{12,20},{14,22},{16,24},... | collective-permute-start | bytes 1769480 | tf_op jit(solution)/shard_map/ppermute | solution.py:112
  447.6 25.4 %collective-permute-start.45 = (f32[96,1536]{1,0:T(8,128)S(1)}, f32[96,1536]{1,0:T(8,128)S(1)}, u32[]{:S(2)}, u32[]{:S(2)}) collective-permute-start(f32[96,1536]{1,0:T(8,128)S(1)} %get-tuple-element.25), channel_id=1, source_target_pairs={{24,16},{26,18},{28,20},{30,22},{16,8},{18,10},{20,12},{22,14},{25... | collective-permute-start | bytes 1769480 | tf_op jit(solution)/shard_map/ppermute | solution.py:112
  449.7 88.6 %collective-permute-start.50 = (f32[96,1536]{1,0:T(8,128)S(1)}, f32[96,1536]{1,0:T(8,128)S(1)}, u32[]{:S(2)}, u32[]{:S(2)}) collective-permute-start(f32[96,1536]{1,0:T(8,128)S(1)} %get-tuple-element.28), channel_id=1, source_target_pairs={{0,8},{2,10},{4,12},{6,14},{8,16},{10,18},{12,20},{14,22},{16,24},... | collective-permute-start | bytes 1769480 | tf_op jit(solution)/shard_map/ppermute | solution.py:112
  492.6 55.3 %collective-permute-start.43 = (f32[96,1536]{1,0:T(8,128)S(1)}, f32[96,1536]{1,0:T(8,128)S(1)}, u32[]{:S(2)}, u32[]{:S(2)}) collective-permute-start(f32[96,1536]{1,0:T(8,128)S(1)} %get-tuple-element.24), channel_id=1, source_target_pairs={{0,8},{2,10},{4,12},{6,14},{8,16},{10,18},{12,20},{14,22},{16,24},... | collective-permute-start | bytes 1769480 | tf_op jit(solution)/shard_map/ppermute | solution.py:112
  500.1 29.0 %collective-permute-start.30 = (f32[96,1536]{1,0:T(8,128)S(1)}, f32[96,1536]{1,0:T(8,128)S(1)}, u32[]{:S(2)}, u32[]{:S(2)}) collective-permute-start(f32[96,1536]{1,0:T(8,128)S(1)} %bitcast_add_fusion.23), channel_id=1, source_target_pairs={{24,16},{26,18},{28,20},{30,22},{16,8},{18,10},{20,12},{22,14},{8,... | collective-permute-start | bytes 1769480 | tf_op jit(solution)/shard_map/ppermute | solution.py:112
  (87 other events, 1401.0 us)

commit v2 on v1

--- a/solution.py
+++ b/solution.py
@@ -96,45 +96,80 @@
         def pick(value, index, axis):
             return lax.dynamic_index_in_dim(value, index, axis, keepdims=False)
 
-        def flow(own, up):
-            got = None
-            for step in range(1, line):
-                if up:
-                    index = jnp.minimum(line - step + row, line - 1)
-                    hops = [(i, i + 1) for i in range(step)]
-                else:
-                    index = jnp.maximum(step - line + row, 0)
-                    hops = [(line - 1 - i, line - 2 - i) for i in range(step)]
-                piece = pick(own, index, 0)
-                if got is not None:
-                    piece = piece + got
-                block = CORES * PAIR
-                got = lax.ppermute(
-                    piece, "dp", [(a * block + k, b * block + k) for a, b in hops for k in range(block)]
-                )
-            return got
-
-        def line_sum(own):
-            if line == 1:
-                return own[0]
-            if line > 4:
-                block = CORES * PAIR
-                groups = [[r * block + k for r in range(line)] for k in range(block)]
-                return lax.psum_scatter(own, "dp", scatter_dimension=0, axis_index_groups=groups)
-            return pick(own, row, 0) + flow(own, True) + flow(own, False)
-
-        def chip_sum(own):
-            got = swap(pick(own, 1 - side, 1), CORES)
-            return line_sum(pick(own, side, 1) + got)
-
-        def expert_sum(grad):
-            own = chip_sum(grad.reshape(line, PAIR, CORES * share, -1)).reshape(CORES, share, -1)
-            return pick(own, core, 0), swap(pick(own, 1 - core, 0), 1)
-
-        def dense_sum(grad):
-            own = grad.reshape(line, PAIR, CORES, share, -1)
-            got = swap(pick(own, 1 - core, 2), 1)
-            return chip_sum(pick(own, core, 2) + got)
+        def cut(value, index, size):
+            return lax.dynamic_slice_in_dim(value, index, size, 1)
+
+        low = row < line // 2
+
+        def hop(value, pairs):
+            block = CORES * PAIR
+            return lax.ppermute(
+                value, "dp", [(a * block + k, b * block + k) for a, b in pairs for k in range(block)]
+            )
+
+        def line_in(own):
+            if line == 4:
+                piece = cut(own, jnp.where(low, 1, 0), 3)
+                return own, (hop(piece, [(0, 1), (3, 2)]),)
+            block = CORES * PAIR
+            groups = [[r * block + k for r in range(line)] for k in range(block)]
+            total = lax.psum_scatter(own, "dp", scatter_dimension=1, axis_index_groups=groups)
+            return own, (total,)
+
+        def line_middle(state, *deps):
+            own, got = state
+            if line == 4:
+                piece = cut(own, jnp.where(low, 2, 0), 2) + cut(got[0], jnp.where(low, 1, 0), 2)
+                got = (*got, hop(after(piece, *deps), [(1, 2), (2, 1)]))
+            return own, got
+
+        def line_out(state, *deps):
+            own, got = state
+            if line == 4:
+                piece = cut(own, jnp.where(low, 0, 3), 1) + cut(got[1], jnp.where(low, 0, 1), 1)
+                got = (*got, hop(after(piece, *deps), [(1, 0), (2, 3)]))
+            return own, got
+
+        def line_end(state):
+            own, got = state
+            if line != 4:
+                return got[0]
+            return (
+                pick(own, row, 1)
+                + pick(got[0], jnp.where(low, 0, 2), 1)
+                + pick(got[1], jnp.where(low, 1, 0), 1)
+                + got[2][:, 0]
+            )
+
+        def after(value, *deps):
+            return lax.optimization_barrier((value, *deps))[0] if deps else value
+
+        def core_swap(rows):
+            rows = rows.reshape(rows.shape[0], CORES, share, -1)
+            return pick(rows, core, 1), swap(pick(rows, 1 - core, 1), 1)
+
+        feature = jnp.arange(width, dtype=jnp.int32)
+        half_width = width // 2
+
+        def chosen_columns(source):
+            return (feature[:, None] == source[None, :]).astype(BF16)
+
+        rest = feature % half_width
+        part_side = jnp.where(feature < half_width, 1 - side, side)
+        pair_order = chosen_columns(
+            (rest // (CORES * share)) * (PAIR * CORES * share)
+            + part_side * (CORES * share)
+            + rest % (CORES * share)
+        )
+        part_core = jnp.where(feature < half_width, 1 - core, core)
+        part_side = jnp.where(rest < half_width // 2, 1 - side, side)
+        rest = rest % (half_width // 2)
+        core_order = chosen_columns(
+            (rest // share) * (PAIR * CORES * share)
+            + part_side * (CORES * share)
+            + part_core * share
+            + rest % share
+        )
 
         segment = segments(seq_lengths[0], count)
         place = jnp.arange(count, dtype=jnp.int32)
@@ -209,17 +244,41 @@
         pre_act = mm("ecd,edf->ecf", dispatch, my_in)
         hidden, gelu_pull = jax.vjp(jax.nn.gelu, pre_act)
         hidden = hidden.astype(BF16)
-        grad_out_rows = mm("ecd,ecf->edf", slot_grad, hidden)
-        out_sums = [expert_sum(grad_out_rows[k]) for k in range(LOCAL)]
-        hidden_grad = mm("ecd,efd->ecf", slot_grad, my_out)
+        units = hidden.shape[2]
+        slot_grad_pair = mm("ecd,dk->eck", slot_grad, pair_order).astype(BF16)
+
+        def grads(left, right):
+            return mm("ecd,ecf->edf", left, right)
+
+        def paired(left, right, got):
+            total = grads(left[:, :, half_width:], right) + got
+            return total.reshape(total.shape[0], line, CORES * share, -1)
+
+        out_first = slot_grad_pair[:1], hidden[:1]
+        out_second = slot_grad_pair[1:], hidden[1:]
+        sent_out_first = grads(out_first[0][:, :, :half_width], out_first[1])
+        got_out_first = swap(sent_out_first, CORES)
+
+        hidden_grad = mm("ecd,efd->ecf", after(slot_grad, sent_out_first), my_out)
         pre_grad = gelu_pull(hidden_grad)[0].astype(BF16)
-        grad_in_rows = mm("ecd,ecf->edf", dispatch, pre_grad)
-        in_sums = [expert_sum(grad_in_rows[k]) for k in range(LOCAL)]
-        expert_part = to_tokens(mm("ecf,efd->ecd", hidden, my_out))
-        back_part = to_tokens(mm("ecf,edf->ecd", pre_grad, my_in))
+        back_slots = mm("ecf,edf->ecd", pre_grad, my_in)
+        part_slots = mm("ecf,efd->ecd", hidden, my_out)
+        back_part = to_tokens(back_slots)
+        expert_part = to_tokens(part_slots)
+        cut_at = units * 2 // 3
+        own = grads(dispatch, after(pre_grad, back_slots)[:, :, cut_at:])
+        state_z = line_in(own.reshape(LOCAL, line, PAIR * CORES * share, -1))
         gate_grad = mp_sum(jnp.sum(grad_seed * expert_part, axis=1, keepdims=True))
         expert_back = mp_sum(back_part)
-        mixed = (middle + gate * mp_sum(expert_part)).astype(BF16)
+        dispatch_pair = mm("ecd,dk->eck", dispatch, pair_order).astype(BF16)
+        in_first = dispatch_pair, pre_grad[:, :, : cut_at // 2]
+        in_second = dispatch_pair, pre_grad[:, :, cut_at // 2 : cut_at]
+
+        sent_out_second = after(
+            grads(out_second[0][:, :, :half_width], out_second[1]), got_out_first, back_part
+        )
+        got_out_second = swap(sent_out_second, CORES)
+        state_a = line_in(after(paired(*out_first, got_out_first), sent_out_second))
 
         logit_grad = (gate_grad * gate * (picked - router)).astype(BF16)
         grad_router = mm("td,te->de", normed_two, logit_grad)
@@ -228,7 +287,6 @@
         middle_grad, grad_gain_two = second_pull(second_grad)
         middle_grad = middle_grad + grad_seed
         attn_grad = middle_grad.astype(BF16)
-        grad_output_rows = mm("td,tc->dc", attn_grad, context)
         context_grad = (
             mm("td,cd->tc", attn_grad, w_output).astype(BF16).reshape(count, heads, HEAD)
         )
@@ -248,14 +306,64 @@
             + mm("tc,dc->td", value_grad, w_value)
         )
         first_grad = mp_sum(first_part)
-        grad_query_rows = mm("td,tc->dc", normed, query_grad)
-        grad_key_rows = mm("td,tc->dc", normed, key_grad)
-        grad_value_rows = mm("td,tc->dc", normed, value_grad)
-        dense = dense_sum(
-            jnp.concatenate(
-                [grad_query_rows, grad_key_rows, grad_value_rows, grad_output_rows], axis=1
+        qkv_grad = jnp.concatenate([query_grad, key_grad, value_grad], axis=1)
+        normed_core = mm("td,dk->tk", normed, core_order).astype(BF16)
+        attn_grad_core = mm("td,dk->tk", attn_grad, core_order).astype(BF16)
+
+        def dense(columns):
+            return jnp.concatenate(
+                [
+                    mm("td,tc->dc", normed_core[:, columns], qkv_grad),
+                    mm("td,tc->dc", attn_grad_core[:, columns], context),
+                ],
+                axis=1,
             )
-        )
+
+        sent_dense = after(dense(slice(0, half_width)), first_part)
+        got_dense = swap(sent_dense, 1)
+
+        state_z = line_middle(state_z, sent_dense)
+        sent_in_first = after(
+            grads(in_first[0][:, :, :half_width], in_first[1]), got_out_second, sent_dense
+        )
+        got_in_first = swap(sent_in_first, CORES)
+        state_b = line_in(after(paired(*out_second, got_out_second), sent_in_first))
+        dense_half = dense(slice(half_width, width)) + got_dense
+        state_a = line_middle(state_a, sent_in_first)
+        mixed_part = after(expert_part, first_grad)
+        mixed = (middle + gate * mp_sum(mixed_part)).astype(BF16)
+        state_z = line_out(state_z, sent_in_first)
+        state_a = line_out(state_a, state_z[1][-1])
+        state_b = line_middle(state_b, state_z[1][-1])
+        sent_in_second = after(
+            grads(in_second[0][:, :, :half_width], in_second[1]), got_in_first, state_z[1][-1]
+        )
+        got_in_second = swap(sent_in_second, CORES)
+        state_c = line_in(after(paired(*in_first, got_in_first), sent_in_second))
+        sums_a = core_swap(line_end(state_a))
+        state_b = line_out(state_b, sent_in_second)
+        sent_late = after(dense_half[: half_width // 2], got_in_second)
+        got_late = swap(sent_late, CORES)
+        state_d = line_in(after(paired(*in_second, got_in_second), sent_late))
+        state_c = line_middle(state_c, sent_late)
+        sums_b = core_swap(line_end(state_b))
+        rows_z = line_end(state_z).reshape(LOCAL, PAIR, CORES * share, -1)
+        got_z = swap(after(pick(rows_z, 1 - side, 1), got_late), CORES)
+        state_e = line_in(
+            (dense_half[half_width // 2 :] + got_late).reshape(1, line, share, -1)
+        )
+        state_c = line_out(state_c, got_late)
+        state_d = line_middle(state_d, got_late)
+        sums_z = core_swap(pick(rows_z, side, 1) + got_z)
+        sums_c = core_swap(line_end(state_c))
+        state_e = line_middle(state_e)
+        state_d = line_out(state_d)
+        state_e = line_out(state_e)
+        sums_d = core_swap(line_end(state_d))
+        dense_sum = line_end(state_e)[0]
+        out_sums = [jnp.concatenate(pair, axis=0) for pair in zip(sums_a, sums_b)]
+        in_sums = [jnp.concatenate(three, axis=2) for three in zip(sums_c, sums_d, sums_z)]
+
         _, first_pull = jax.vjp(norm_rows, inputs, gain_one)
         input_grad, _ = first_pull(first_grad)
         grad_tokens = middle_grad + input_grad
@@ -274,8 +382,7 @@
         small = lax.dynamic_slice_in_dim(small[: 2 + E], device * share, share, 1)
 
         def by_expert(sums):
-            mine = jnp.stack([own for own, _ in sums])
-            other = jnp.stack([got for _, got in sums])
+            mine, other = sums
             first = core == 0
             return jnp.concatenate(
                 [jnp.where(first, mine, other), jnp.where(first, other, mine)], axis=0
@@ -285,10 +392,10 @@
             mixed,
             grad_tokens,
             small[0],
-            dense[:, :inner],
-            dense[:, inner : 2 * inner],
-            dense[:, 2 * inner : 3 * inner],
-            dense[:, 3 * inner :].T,
+            dense_sum[:, :inner],
+            dense_sum[:, inner : 2 * inner],
+            dense_sum[:, 2 * inner : 3 * inner],
+            dense_sum[:, 3 * inner :].T,
             table_total,
             small[1],
             small[2:].T,

time: 588 us -> 392 us (0.67)
  waiting for transfers between devices: 313 us -> 193 us
  starting transfers between devices: 114 us -> 63.2 us
  local copies, waits for them, and re-layouts: 42.1 us -> 14.3 us
    ppermute x20 -> x22, waiting for transfers between devices: 189 us -> 64.1 us  [swap(): return lax.ppermute(value, 'dp', [(i, i ^ stride) for i in range(n_dp)])]
    ppermute x30 -> x18, starting transfers between devices: 88.8 us -> 39.7 us  [hop(): lax.ppermute(value, 'dp', [(a * block + k, b * block + k) for a, b in pai...]
    ppermute x6, waiting for transfers between devices: 36.3 us -> 78.8 us  [mp_other(): return lax.ppermute(value, 'mp', [(0, 1), (1, 0)])]
    ppermute x30 -> x18, waiting for transfers between devices: 88.5 us -> 50.5 us  [hop(): lax.ppermute(value, 'dp', [(a * block + k, b * block + k) for a, b in pai...]
    squeeze x11 -> x6, local copies, waits for them, and re-layouts: 13.6 us -> 0.24 us  [pick(): return lax.dynamic_index_in_dim(value, index, axis, keepdims=False)]
    slice x2 -> x1, local copies, waits for them, and re-layouts: 9.82 us -> 0.08 us  [shards(): sent_late = after(dense_half[:half_width // 2], got_in_second)]
    concatenate x1 -> x2, local copies, waits for them, and re-layouts: 6.07 us -> 0.04 us  [the longest x1 0.02 us: shards(): out_sums = [jnp.concatenate(pair, axis=0) for pair in zip(sums_a, sums_b)]]
    dot_general x33 -> x44, matrix products: 71 us -> 76.5 us  [mm(): jnp.einsum(spec, left, right, preferred_element_type=F32, precision=preci...]
  transfers between devices with their start and end apart: 56 -> 46, of which waited for: 25 -> 20; matrix products, arithmetic and copies ran while one was open for 18% -> 22% of each run, Pallas kernels for 0% -> 0%
where the time goes in v2:
time: 392 us; the launch traced here: 385 us
  waiting for transfers between devices  193 us (49%)
  matrix products  76.5 us (20%)
  starting transfers between devices  63.2 us (16%)
  other arithmetic  35 us (9%)
  local copies, waits for them, and re-layouts  14.3 us (4%)
    ppermute x6, waiting for transfers between devices, mp_other(): return lax.ppermute(value, 'mp', [(0, 1), (1, 0)])  78.8 us
    dot_general x44, matrix products, mm(): jnp.einsum(spec, left, right, preferred_element_type=F32, precision=preci...  76.5 us
    ppermute x22, waiting for transfers between devices, swap(): return lax.ppermute(value, 'dp', [(i, i ^ stride) for i in range(n_dp)])  64.1 us
    ppermute x18, waiting for transfers between devices, hop(): lax.ppermute(value, 'dp', [(a * block + k, b * block + k) for a, b in pai...  50.5 us
    ppermute x18, starting transfers between devices, hop(): lax.ppermute(value, 'dp', [(a * block + k, b * block + k) for a, b in pai...  39.7 us
    ppermute x22, starting transfers between devices, swap(): return lax.ppermute(value, 'dp', [(i, i ^ stride) for i in range(n_dp)])  13.7 us
    ppermute x6, starting transfers between devices, mp_other(): return lax.ppermute(value, 'mp', [(0, 1), (1, 0)])  9.82 us
    unnamed x125, local copies, waits for them, and re-layouts  8.78 us
  transfers between devices with their start and end apart: 46, of which 20 were waited for; matrix products, arithmetic and copies ran while one was open for 22% of the time, Pallas kernels for 0%

profile of v2, /device:TPU:0, one launch (start us, length us, event | category | flops | bytes accessed | tf_op | source)
XLA Modules:
  0.0 385.1 jit_solution(3409736429961312036)
XLA Ops:
  7.0 5.1 %fusion.1 = f32[512,512,6]{0,2,1:T(8,128)S(1)} fusion(s32[512,512]{0,1:T(8,128)S(1)} %fusion.60, bf16[32,6]{0,1:T(8,128)(2,1)S(1)} %copy-done.53), kind=kOutput, calls=%fused_computation.2 | convolution fusion | flops 109051904 | bytes 7340416 | tf_op jit(solution)/shard_map/qkb,bh->hqk/dot_general | solution.py:46
  12.2 4.7 %fusion.157 = (f32[6,512]{1,0:T(8,128)S(1)}, f32[6,512,512]{1,2,0:T(8,128)S(1)}) fusion(f32[512,512,6]{0,2,1:T(8,128)S(1)} %fusion.1, bf16[512,6,64]{0,2,1:T(8,128)(2,1)S(1)} %bitcast.221, bf16[512,6,64]{0,2,1:T(8,128)(2,1)S(1)} %bitcast.223, pred[512,512]{0,1:T(8,128)(4,1)S(1)} %broadcast_compare_fusion), kind=kOutput, calls=%fused_computation.287 | convolution fusion | flops 206042112 | bytes 13643776 | tf_op jit(solution)/shard_map/qhd,khd->hqk/dot_general | solution.py:46
  21.3 3.0 collective-permute-start
  26.4 32.4 %collective-permute-done = f32[512,768]{1,0:T(8,128)} collective-permute-done((f32[512,768]{1,0:T(8,128)S(1)}, f32[512,768]{1,0:T(8,128)}, u32[]{:S(2)}, u32[]{:S(2)}) %collective-permute-start) | collective-permute-done | bytes 1572896 | tf_op jit(solution)/shard_map/ppermute | solution.py:57
  74.7 4.3 %multiply_convert_fusion.1 = (bf16[2,320,1536]{2,1,0:T(8,128)(2,1)S(1)}, f32[2,320,1536]{2,1,0:T(8,128)S(1)}) fusion(bf16[4,768,1536]{2,1,0:T(8,128)(2,1)} %param.23, s32[]{:T(128)S(6)} %select_n.322, bf16[2,160,768]{2,1,0:T(8,128)(2,1)S(1)} %bitcast.212, bf16[2,160,768]{2,1,0:T(8,128)(2,1)S(1)} %bitcast.209), kind=kOutput, calls=%fused_computation.30 | convolution fusion | flops 1520762880 | bytes 11599876 | tf_op jit(solution)/shard_map/ecd,edf->ecf/dot_general | solution.py:46
  83.3 4.1 %fusion.21 = bf16[2,320,1536]{2,1,0:T(8,128)(2,1)S(1)} fusion(f32[2,320,1536]{2,1,0:T(8,128)S(1)} %get-tuple-element.102, bf16[2,320,768]{2,1,0:T(8,128)(2,1)S(1)} %pad_maximum_fusion.6, bf16[4,1536,768]{2,1,0:T(8,128)(2,1)S(1)} %bitcast.243, s32[]{:T(128)S(6)} %select_n.322), kind=kOutput, calls=%fused_computation.29 | convolution fusion | flops 1529610240 | bytes 11599876 | tf_op jit(solution)/shard_map/ecd,efd->ecf/dot_general | solution.py:46
  87.4 4.8 %fusion.11 = f32[2,320,768]{2,1,0:T(8,128)S(1)} fusion(bf16[2,320,1536]{2,1,0:T(8,128)(2,1)S(1)} %fusion.21, bf16[4,768,1536]{2,1,0:T(8,128)(2,1)} %param.23, s32[]{:T(128)S(6)} %select_n.322), kind=kOutput, calls=%fused_computation.19 | convolution fusion | flops 1509949440 | bytes 8650756 | tf_op jit(solution)/shard_map/ecf,edf->ecd/dot_general | solution.py:46
  94.5 3.6 collective-permute-start.20
  107.3 2.8 fusion.37
  112.7 28.0 %collective-permute-done.8 = f32[512,1]{0,1:T(1,128)S(1)} collective-permute-done((f32[512,1]{0,1:T(1,128)S(1)}, f32[512,1]{0,1:T(1,128)S(1)}, u32[]{:S(2)}, u32[]{:S(2)}) %collective-permute-start.8) | collective-permute-done | bytes 2080 | tf_op jit(solution)/shard_map/ppermute | solution.py:57
  145.1 2.8 collective-permute-start.38
  173.8 9.5 %fusion.57 = f32[6,32]{1,0:T(8,128)S(1)} fusion(s32[512,512]{0,1:T(8,128)} %copy-done.14, bf16[6,512,512]{1,2,0:T(8,128)(2,1)} %copy-done.3), kind=kOutput, calls=%fused_computation.105 | convolution fusion | flops 109051904 | bytes 4195072 | tf_op jit(solution)/shard_map/hqk,qkb->bh/dot_general | solution.py:46
  185.3 16.8 %collective-permute-done.9 = f32[512,768]{1,0:T(8,128)} collective-permute-done((f32[512,768]{1,0:T(8,128)}, f32[512,768]{1,0:T(8,128)}, u32[]{:S(2)}, u32[]{:S(2)}) %collective-permute-start.9) | collective-permute-done | bytes 1572896 | tf_op jit(solution)/shard_map/ppermute | solution.py:57
  220.2 3.1 collective-permute-start.15
  228.7 4.1 %collective-permute-start.41 = (f32[1,3,96,1536]{3,2,1,0:T(8,128)S(1)}, f32[1,3,96,1536]{3,2,1,0:T(8,128)S(1)}, u32[]{:S(2)}, u32[]{:S(2)}) collective-permute-start(f32[1,3,96,1536]{3,2,1,0:T(8,128)S(1)} %constant_dynamic-slice_fusion), channel_id=1, source_target_pairs={{0,8},{2,10},{4,12},{6,14},{24,16},{26,18},{28,20},{30,22},{1,9},{... | collective-permute-start | bytes 5308424 | tf_op jit(solution)/shard_map/ppermute | solution.py:106
  238.6 12.6 %collective-permute-done.22 = f32[2,1,192,512]{3,2,1,0:T(8,128)S(1)} collective-permute-done((f32[2,1,192,512]{3,2,1,0:T(8,128)S(1)}, f32[2,1,192,512]{3,2,1,0:T(8,128)S(1)}, u32[]{:S(2)}, u32[]{:S(2)}) %collective-permute-start.22) | collective-permute-done | bytes 786464 | tf_op jit(solution)/shard_map/ppermute | solution.py:106
  254.5 12.9 %collective-permute-done.19 = f32[2,384,512]{2,1,0:T(8,128)S(1)} collective-permute-done((f32[2,384,512]{2,1,0:T(8,128)S(1)}, f32[2,384,512]{2,1,0:T(8,128)S(1)}, u32[]{:S(2)}, u32[]{:S(2)}) %collective-permute-start.19) | collective-permute-done | bytes 1572896 | tf_op jit(solution)/shard_map/ppermute | solution.py:54
  271.2 6.4 %collective-permute-start.28 = (f32[2,3,96,512]{3,2,1,0:T(8,128)S(1)}, f32[2,3,96,512]{3,2,1,0:T(8,128)S(1)}, u32[]{:S(2)}, u32[]{:S(2)}) collective-permute-start(f32[2,3,96,512]{3,2,1,0:T(8,128)S(1)} %constant_dynamic-slice_fusion.2), channel_id=1, source_target_pairs={{0,8},{2,10},{4,12},{6,14},{24,16},{26,18},{28,20},{30,22},{1,9},{... | collective-permute-start | bytes 3538952 | tf_op jit(solution)/shard_map/ppermute | solution.py:106
  280.4 21.6 %collective-permute-done.23 = f32[2,384,512]{2,1,0:T(8,128)S(1)} collective-permute-done((f32[2,384,512]{2,1,0:T(8,128)S(1)}, f32[2,384,512]{2,1,0:T(8,128)S(1)}, u32[]{:S(2)}, u32[]{:S(2)}) %collective-permute-start.23) | collective-permute-done | bytes 1572896 | tf_op jit(solution)/shard_map/ppermute | solution.py:54
  306.8 17.6 %collective-permute-done.24 = f32[192,1536]{1,0:T(8,128)S(1)} collective-permute-done((f32[192,1536]{1,0:T(8,128)S(1)}, f32[192,1536]{1,0:T(8,128)S(1)}, u32[]{:S(2)}, u32[]{:S(2)}) %collective-permute-start.24) | collective-permute-done | bytes 1179680 | tf_op jit(solution)/shard_map/ppermute | solution.py:54
  326.7 7.4 %collective-permute-start.25 = (f32[1,3,48,1536]{3,2,1,0:T(8,128)S(1)}, f32[1,3,48,1536]{3,2,1,0:T(8,128)S(1)}, u32[]{:S(2)}, u32[]{:S(2)}) collective-permute-start(f32[1,3,48,1536]{3,2,1,0:T(8,128)S(1)} %constant_dynamic-slice_fusion.4), channel_id=1, source_target_pairs={{0,8},{2,10},{4,12},{6,14},{24,16},{26,18},{28,20},{30,22},{1,9},{... | collective-permute-start | bytes 2654216 | tf_op jit(solution)/shard_map/ppermute | solution.py:106
  338.5 5.5 %collective-permute-done.34 = f32[2,96,512]{2,1,0:T(8,128)S(1)} collective-permute-done((f32[2,96,512]{2,1,0:T(8,128)S(1)}, f32[2,96,512]{2,1,0:T(8,128)S(1)}, u32[]{:S(2)}, u32[]{:S(2)}) %collective-permute-start.34) | collective-permute-done | bytes 393248 | tf_op jit(solution)/shard_map/ppermute | solution.py:54
  344.2 13.9 %collective-permute-done.33 = f32[2,1,96,512]{3,2,1,0:T(8,128)S(1)} collective-permute-done((f32[2,1,96,512]{3,2,1,0:T(8,128)S(1)}, f32[2,1,96,512]{3,2,1,0:T(8,128)S(1)}, u32[]{:S(2)}, u32[]{:S(2)}) %collective-permute-start.33) | collective-permute-done | bytes 393248 | tf_op jit(solution)/shard_map/ppermute | solution.py:106
  362.9 20.9 %collective-permute-done.27 = f32[1,1,48,1536]{3,2,1,0:T(8,128)S(1)} collective-permute-done((f32[1,1,48,1536]{3,2,1,0:T(8,128)S(1)}, f32[1,1,48,1536]{3,2,1,0:T(8,128)S(1)}, u32[]{:S(2)}, u32[]{:S(2)}) %collective-permute-start.27) | collective-permute-done | bytes 294944 | tf_op jit(solution)/shard_map/ppermute | solution.py:106
  (333 shorter events, 134.6 us)
Async XLA Ops:
  21.3 37.5 %collective-permute-start = (f32[512,768]{1,0:T(8,128)S(1)}, f32[512,768]{1,0:T(8,128)}, u32[]{:S(2)}, u32[]{:S(2)}) collective-permute-start(f32[512,768]{1,0:T(8,128)S(1)} %fusion.159), channel_id=1, source_target_pairs={{0,1},{1,0},{2,3},{3,2},{4,5},{5,4},{6,7},{7,6},{8,9},{9,8},{10,11... | collective-permute-start | bytes 4718600 | tf_op jit(solution)/shard_map/ppermute | solution.py:57
  81.5 59.5 %collective-permute-start.17 = (f32[1,384,1536]{2,1,0:T(8,128)S(1)}, f32[1,384,1536]{2,1,0:T(8,128)S(1)}, u32[]{:S(2)}, u32[]{:S(2)}) collective-permute-start(f32[1,384,1536]{2,1,0:T(8,128)S(1)} %convolution_bitcast_fusion.3), channel_id=1, source_target_pairs={{0,4},{2,6},{4,0},{6,2},{8,12},{10,14},{12,8},{14,10},{16,20},{18,... | collective-permute-start | bytes 7077896 | tf_op jit(solution)/shard_map/ppermute | solution.py:54
  94.5 55.1 %collective-permute-start.20 = (f32[2,3,192,512]{3,2,1,0:T(8,128)S(1)}, f32[2,3,192,512]{3,2,1,0:T(8,128)S(1)}, u32[]{:S(2)}, u32[]{:S(2)}) collective-permute-start(f32[2,3,192,512]{3,2,1,0:T(8,128)S(1)} %constant_dynamic-slice_fusion.5), channel_id=1, source_target_pairs={{0,8},{2,10},{4,12},{6,14},{24,16},{26,18},{28,20},{30,22},{1,9},{... | collective-permute-start | bytes 7077896 | tf_op jit(solution)/shard_map/ppermute | solution.py:106
  104.5 47.0 %collective-permute-start.7 = (f32[512,768]{1,0:T(8,128)S(1)}, f32[512,768]{1,0:T(8,128)S(1)}, u32[]{:S(2)}, u32[]{:S(2)}) collective-permute-start(f32[512,768]{1,0:T(8,128)S(1)} %fusion.49), channel_id=1, source_target_pairs={{0,1},{1,0},{2,3},{3,2},{4,5},{5,4},{6,7},{7,6},{8,9},{9,8},{10,11... | collective-permute-start | bytes 4718600 | tf_op jit(solution)/shard_map/ppermute | solution.py:57
  110.1 30.7 %collective-permute-start.8 = (f32[512,1]{0,1:T(1,128)S(1)}, f32[512,1]{0,1:T(1,128)S(1)}, u32[]{:S(2)}, u32[]{:S(2)}) collective-permute-start(f32[512,1]{0,1:T(1,128)S(1)} %bitcast.240), channel_id=1, source_target_pairs={{0,1},{1,0},{2,3},{3,2},{4,5},{5,4},{6,7},{7,6},{8,9},{9,8},{10,11... | collective-permute-start | bytes 6152 | tf_op jit(solution)/shard_map/ppermute | solution.py:57
  140.9 85.0 %collective-permute-start.18 = (f32[1,384,1536]{2,1,0:T(8,128)}, f32[1,384,1536]{2,1,0:T(8,128)}, u32[]{:S(2)}, u32[]{:S(2)}) collective-permute-start(f32[1,384,1536]{2,1,0:T(8,128)} %convolution_bitcast_fusion.2), channel_id=1, source_target_pairs={{0,4},{2,6},{4,0},{6,2},{8,12},{10,14},{12,8},{14,10},{16,20},{18,... | collective-permute-start | bytes 7077896 | tf_op jit(solution)/shard_map/ppermute | solution.py:54
  145.1 70.3 %collective-permute-start.38 = (f32[1,3,96,1536]{3,2,1,0:T(8,128)}, f32[1,3,96,1536]{3,2,1,0:T(8,128)}, u32[]{:S(2)}, u32[]{:S(2)}) collective-permute-start(f32[1,3,96,1536]{3,2,1,0:T(8,128)} %constant_dynamic-slice_fusion.3), channel_id=1, source_target_pairs={{0,8},{2,10},{4,12},{6,14},{24,16},{26,18},{28,20},{30,22},{1,9},{... | collective-permute-start | bytes 5308424 | tf_op jit(solution)/shard_map/ppermute | solution.py:106
  167.1 35.0 %collective-permute-start.9 = (f32[512,768]{1,0:T(8,128)}, f32[512,768]{1,0:T(8,128)}, u32[]{:S(2)}, u32[]{:S(2)}) collective-permute-start(f32[512,768]{1,0:T(8,128)} %add_add_fusion.2), channel_id=1, source_target_pairs={{0,1},{1,0},{2,3},{3,2},{4,5},{5,4},{6,7},{7,6},{8,9},{9,8},{10,11... | collective-permute-start | bytes 4718600 | tf_op jit(solution)/shard_map/ppermute | solution.py:57
  171.6 63.7 %collective-permute-start.16 = (f32[384,1536]{1,0:T(8,128)}, f32[384,1536]{1,0:T(8,128)}, u32[]{:S(2)}, u32[]{:S(2)}) collective-permute-start(f32[384,1536]{1,0:T(8,128)} %pad_maximum_fusion), channel_id=1, source_target_pairs={{0,2},{2,0},{4,6},{6,4},{8,10},{10,8},{12,14},{14,12},{16,18},{18,... | collective-permute-start | bytes 7077896 | tf_op jit(solution)/shard_map/ppermute | solution.py:54
  171.6 51.6 %collective-permute-start.21 = (f32[2,2,192,512]{3,2,1,0:T(8,128)}, f32[2,2,192,512]{3,2,1,0:T(8,128)}, u32[]{:S(2)}, u32[]{:S(2)}) collective-permute-start(f32[2,2,192,512]{3,2,1,0:T(8,128)} %dynamic-slice_add_fusion), channel_id=1, source_target_pairs={{8,16},{10,18},{12,20},{14,22},{16,8},{18,10},{20,12},{22,14},{9,1... | collective-permute-start | bytes 4718600 | tf_op jit(solution)/shard_map/ppermute | solution.py:106
  213.9 55.4 %collective-permute-start.10 = (f32[512,768]{1,0:T(8,128)S(1)}, f32[512,768]{1,0:T(8,128)S(1)}, u32[]{:S(2)}, u32[]{:S(2)}) collective-permute-start(f32[512,768]{1,0:T(8,128)S(1)} %copy-done.17), channel_id=1, source_target_pairs={{0,1},{1,0},{2,3},{3,2},{4,5},{5,4},{6,7},{7,6},{8,9},{9,8},{10,11... | collective-permute-start | bytes 4718600 | tf_op jit(solution)/shard_map/ppermute | solution.py:57
  228.7 39.3 %collective-permute-start.41 = (f32[1,3,96,1536]{3,2,1,0:T(8,128)S(1)}, f32[1,3,96,1536]{3,2,1,0:T(8,128)S(1)}, u32[]{:S(2)}, u32[]{:S(2)}) collective-permute-start(f32[1,3,96,1536]{3,2,1,0:T(8,128)S(1)} %constant_dynamic-slice_fusion), channel_id=1, source_target_pairs={{0,8},{2,10},{4,12},{6,14},{24,16},{26,18},{28,20},{30,22},{1,9},{... | collective-permute-start | bytes 5308424 | tf_op jit(solution)/shard_map/ppermute | solution.py:106
  232.9 34.6 %collective-permute-start.19 = (f32[2,384,512]{2,1,0:T(8,128)S(1)}, f32[2,384,512]{2,1,0:T(8,128)S(1)}, u32[]{:S(2)}, u32[]{:S(2)}) collective-permute-start(f32[2,384,512]{2,1,0:T(8,128)S(1)} %copy-done.38), channel_id=1, source_target_pairs={{0,4},{2,6},{4,0},{6,2},{8,12},{10,14},{12,8},{14,10},{16,20},{18,... | collective-permute-start | bytes 4718600 | tf_op jit(solution)/shard_map/ppermute | solution.py:54
  235.3 17.7 %collective-permute-start.39 = (f32[1,2,96,1536]{3,2,1,0:T(8,128)S(1)}, f32[1,2,96,1536]{3,2,1,0:T(8,128)S(1)}, u32[]{:S(2)}, u32[]{:S(2)}) collective-permute-start(f32[1,2,96,1536]{3,2,1,0:T(8,128)S(1)} %dynamic-slice_add_fusion.2), channel_id=1, source_target_pairs={{8,16},{10,18},{12,20},{14,22},{16,8},{18,10},{20,12},{22,14},{9,1... | collective-permute-start | bytes 3538952 | tf_op jit(solution)/shard_map/ppermute | solution.py:106
  253.1 24.6 %collective-permute-start.40 = (f32[1,1,96,1536]{3,2,1,0:T(8,128)S(1)}, f32[1,1,96,1536]{3,2,1,0:T(8,128)S(1)}, u32[]{:S(2)}, u32[]{:S(2)}) collective-permute-start(f32[1,1,96,1536]{3,2,1,0:T(8,128)S(1)} %dynamic-slice_add_fusion.7), channel_id=1, source_target_pairs={{8,0},{10,2},{12,4},{14,6},{16,24},{18,26},{20,28},{22,30},{9,1},{... | collective-permute-start | bytes 1769480 | tf_op jit(solution)/shard_map/ppermute | solution.py:106
  267.5 34.6 %collective-permute-start.23 = (f32[2,384,512]{2,1,0:T(8,128)S(1)}, f32[2,384,512]{2,1,0:T(8,128)S(1)}, u32[]{:S(2)}, u32[]{:S(2)}) collective-permute-start(f32[2,384,512]{2,1,0:T(8,128)S(1)} %copy-done.37), channel_id=1, source_target_pairs={{0,4},{2,6},{4,0},{6,2},{8,12},{10,14},{12,8},{14,10},{16,20},{18,... | collective-permute-start | bytes 4718600 | tf_op jit(solution)/shard_map/ppermute | solution.py:54
  271.2 33.8 %collective-permute-start.28 = (f32[2,3,96,512]{3,2,1,0:T(8,128)S(1)}, f32[2,3,96,512]{3,2,1,0:T(8,128)S(1)}, u32[]{:S(2)}, u32[]{:S(2)}) collective-permute-start(f32[2,3,96,512]{3,2,1,0:T(8,128)S(1)} %constant_dynamic-slice_fusion.2), channel_id=1, source_target_pairs={{0,8},{2,10},{4,12},{6,14},{24,16},{26,18},{28,20},{30,22},{1,9},{... | collective-permute-start | bytes 3538952 | tf_op jit(solution)/shard_map/ppermute | solution.py:106
  279.0 25.8 %collective-permute-start.43 = (f32[1,1,96,1536]{3,2,1,0:T(8,128)S(1)}, f32[1,1,96,1536]{3,2,1,0:T(8,128)S(1)}, u32[]{:S(2)}, u32[]{:S(2)}) collective-permute-start(f32[1,1,96,1536]{3,2,1,0:T(8,128)S(1)} %dynamic-slice_add_fusion.6), channel_id=1, source_target_pairs={{8,0},{10,2},{12,4},{14,6},{16,24},{18,26},{20,28},{22,30},{9,1},{... | collective-permute-start | bytes 1769480 | tf_op jit(solution)/shard_map/ppermute | solution.py:106
  280.3 25.6 %collective-permute-start.44 = (f32[1,48,1536]{2,1,0:T(8,128)S(1)}, f32[1,48,1536]{2,1,0:T(8,128)S(1)}, u32[]{:S(2)}, u32[]{:S(2)}) collective-permute-start(f32[1,48,1536]{2,1,0:T(8,128)S(1)} %get-tuple-element.78), channel_id=1, source_target_pairs={{0,2},{2,0},{4,6},{6,4},{8,10},{10,8},{12,14},{14,12},{16,18},{18,... | collective-permute-start | bytes 884744 | tf_op jit(solution)/shard_map/ppermute | solution.py:54
  302.0 22.3 %collective-permute-start.24 = (f32[192,1536]{1,0:T(8,128)S(1)}, f32[192,1536]{1,0:T(8,128)S(1)}, u32[]{:S(2)}, u32[]{:S(2)}) collective-permute-start(f32[192,1536]{1,0:T(8,128)S(1)} %slice.176), channel_id=1, source_target_pairs={{0,4},{2,6},{4,0},{6,2},{8,12},{10,14},{12,8},{14,10},{16,20},{18,... | collective-permute-start | bytes 3538952 | tf_op jit(solution)/shard_map/ppermute | solution.py:54
  303.3 22.3 %collective-permute-start.31 = (f32[2,3,96,512]{3,2,1,0:T(8,128)S(1)}, f32[2,3,96,512]{3,2,1,0:T(8,128)S(1)}, u32[]{:S(2)}, u32[]{:S(2)}) collective-permute-start(f32[2,3,96,512]{3,2,1,0:T(8,128)S(1)} %constant_dynamic-slice_fusion.1), channel_id=1, source_target_pairs={{0,8},{2,10},{4,12},{6,14},{24,16},{26,18},{28,20},{30,22},{1,9},{... | collective-permute-start | bytes 3538952 | tf_op jit(solution)/shard_map/ppermute | solution.py:106
  326.7 31.7 %collective-permute-start.25 = (f32[1,3,48,1536]{3,2,1,0:T(8,128)S(1)}, f32[1,3,48,1536]{3,2,1,0:T(8,128)S(1)}, u32[]{:S(2)}, u32[]{:S(2)}) collective-permute-start(f32[1,3,48,1536]{3,2,1,0:T(8,128)S(1)} %constant_dynamic-slice_fusion.4), channel_id=1, source_target_pairs={{0,8},{2,10},{4,12},{6,14},{24,16},{26,18},{28,20},{30,22},{1,9},{... | collective-permute-start | bytes 2654216 | tf_op jit(solution)/shard_map/ppermute | solution.py:106
  337.2 20.9 %collective-permute-start.33 = (f32[2,1,96,512]{3,2,1,0:T(8,128)S(1)}, f32[2,1,96,512]{3,2,1,0:T(8,128)S(1)}, u32[]{:S(2)}, u32[]{:S(2)}) collective-permute-start(f32[2,1,96,512]{3,2,1,0:T(8,128)S(1)} %dynamic-slice_add_fusion.9), channel_id=1, source_target_pairs={{8,0},{10,2},{12,4},{14,6},{16,24},{18,26},{20,28},{22,30},{9,1},{... | collective-permute-start | bytes 1179656 | tf_op jit(solution)/shard_map/ppermute | solution.py:106
  360.0 23.8 %collective-permute-start.27 = (f32[1,1,48,1536]{3,2,1,0:T(8,128)S(1)}, f32[1,1,48,1536]{3,2,1,0:T(8,128)S(1)}, u32[]{:S(2)}, u32[]{:S(2)}) collective-permute-start(f32[1,1,48,1536]{3,2,1,0:T(8,128)S(1)} %dynamic-slice_add_fusion.11), channel_id=1, source_target_pairs={{8,0},{10,2},{12,4},{14,6},{16,24},{18,26},{20,28},{22,30},{9,1},{... | collective-permute-start | bytes 884744 | tf_op jit(solution)/shard_map/ppermute | solution.py:106
  (84 other events, 671.4 us)

commit v3 on v1

--- a/solution.py
+++ b/solution.py
@@ -9,6 +9,7 @@
 CAP = 160
 CORES = 2
 PAIR = 2
+LINE = 2
 LOCAL = E // CORES
 
 EPS = 1e-06
@@ -48,7 +49,7 @@
 
 def solution(mesh):
     n_dp, n_mp = mesh.shape["dp"], mesh.shape["mp"]
-    line = n_dp // (CORES * PAIR)
+    bits = n_dp.bit_length() - 1
 
     def swap(value, stride):
         return lax.ppermute(value, "dp", [(i, i ^ stride) for i in range(n_dp)])
@@ -58,15 +59,6 @@
 
     def mp_sum(value):
         return value + mp_other(value) if n_mp == 2 else lax.psum(value, "mp")
-
-    def dp_sum(value):
-        if n_dp & (n_dp - 1):
-            return lax.psum(value, "dp")
-        stride = 1
-        while stride < n_dp:
-            value = value + swap(value, stride)
-            stride *= 2
-        return value
 
     def shards(
         tokens,
@@ -86,55 +78,57 @@
     ):
         device = lax.axis_index("dp")
         core = device % CORES
-        side = (device // CORES) % PAIR
-        row = device // (CORES * PAIR)
         count, width = tokens.shape
         share = width // n_dp
         heads = position_table.shape[1]
         inner = heads * HEAD
 
-        def pick(value, index, axis):
-            return lax.dynamic_index_in_dim(value, index, axis, keepdims=False)
-
-        def flow(own, up):
-            got = None
-            for step in range(1, line):
-                if up:
-                    index = jnp.minimum(line - step + row, line - 1)
-                    hops = [(i, i + 1) for i in range(step)]
-                else:
-                    index = jnp.maximum(step - line + row, 0)
-                    hops = [(line - 1 - i, line - 2 - i) for i in range(step)]
-                piece = pick(own, index, 0)
-                if got is not None:
-                    piece = piece + got
-                block = CORES * PAIR
-                got = lax.ppermute(
-                    piece, "dp", [(a * block + k, b * block + k) for a, b in hops for k in range(block)]
-                )
+        last = []
+
+        def after(value, *deps):
+            return lax.optimization_barrier((value, *deps))[0] if deps else value
+
+        def ready(value):
+            value = after(value, *last)
+            last[:] = [value]
+            return value
+
+        def take(got):
+            got = after(got, *last)
+            last[:] = [got]
             return got
 
-        def line_sum(own):
-            if line == 1:
-                return own[0]
-            if line > 4:
-                block = CORES * PAIR
-                groups = [[r * block + k for r in range(line)] for k in range(block)]
-                return lax.psum_scatter(own, "dp", scatter_dimension=0, axis_index_groups=groups)
-            return pick(own, row, 0) + flow(own, True) + flow(own, False)
-
-        def chip_sum(own):
-            got = swap(pick(own, 1 - side, 1), CORES)
-            return line_sum(pick(own, side, 1) + got)
-
-        def expert_sum(grad):
-            own = chip_sum(grad.reshape(line, PAIR, CORES * share, -1)).reshape(CORES, share, -1)
-            return pick(own, core, 0), swap(pick(own, 1 - core, 0), 1)
-
-        def dense_sum(grad):
-            own = grad.reshape(line, PAIR, CORES, share, -1)
-            got = swap(pick(own, 1 - core, 2), 1)
-            return chip_sum(pick(own, core, 2) + got)
+        def begin(rows, bit):
+            half = rows.shape[1] // 2
+            return rows[:, half:], swap(ready(rows[:, :half]), 1 << bit)
+
+        def finish(state):
+            kept, got = state
+            return kept + take(got)
+
+        def line_next(state):
+            for bit in range(LINE + 1, bits - 1):
+                state = begin(finish(state), bit)
+            return begin(finish(state), bits - 1)
+
+        def core_begin(state):
+            return begin(finish(state), 0)
+
+        feature = jnp.arange(width, dtype=jnp.int32)
+        half_width = width // 2
+
+        def column_order(names):
+            source = feature % share
+            for place, name in enumerate(names):
+                same = (feature // share) >> (bits - 1 - place) & 1
+                bit = (device >> name & 1) ^ (1 - same)
+                source = source + (bit << name) * share
+            return (feature[:, None] == source[None, :]).astype(BF16)
+
+        line_bits = list(range(LINE, bits))
+        pair_order = column_order([1, *line_bits, 0])
+        line_order = column_order([*line_bits, 1, 0])
+        core_order = column_order([0, 1, *line_bits])
 
         segment = segments(seq_lengths[0], count)
         place = jnp.arange(count, dtype=jnp.int32)
@@ -209,17 +203,46 @@
         pre_act = mm("ecd,edf->ecf", dispatch, my_in)
         hidden, gelu_pull = jax.vjp(jax.nn.gelu, pre_act)
         hidden = hidden.astype(BF16)
-        grad_out_rows = mm("ecd,ecf->edf", slot_grad, hidden)
-        out_sums = [expert_sum(grad_out_rows[k]) for k in range(LOCAL)]
-        hidden_grad = mm("ecd,efd->ecf", slot_grad, my_out)
+        units = hidden.shape[2]
+        slot_grad_pair = mm("ecd,dk->eck", slot_grad, pair_order).astype(BF16)
+
+        def grads(left, right):
+            return mm("ecd,ecf->edf", left, right)
+
+        def paired(pair, got):
+            return grads(pair[0][:, :, mine], pair[1]) + take(got)
+
+        out_first = slot_grad_pair[:1], hidden[:1]
+        out_second = slot_grad_pair[1:], hidden[1:]
+        other, mine = slice(0, half_width), slice(half_width, width)
+
+        def sent_part(pair):
+            return grads(pair[0][:, :, other], pair[1])
+
+        got_a = swap(ready(sent_part(out_first)), PAIR)
+        hidden_grad = mm("ecd,efd->ecf", after(slot_grad, *last), my_out)
         pre_grad = gelu_pull(hidden_grad)[0].astype(BF16)
-        grad_in_rows = mm("ecd,ecf->edf", dispatch, pre_grad)
-        in_sums = [expert_sum(grad_in_rows[k]) for k in range(LOCAL)]
-        expert_part = to_tokens(mm("ecf,efd->ecd", hidden, my_out))
-        back_part = to_tokens(mm("ecf,edf->ecd", pre_grad, my_in))
-        gate_grad = mp_sum(jnp.sum(grad_seed * expert_part, axis=1, keepdims=True))
-        expert_back = mp_sum(back_part)
-        mixed = (middle + gate * mp_sum(expert_part)).astype(BF16)
+        back_slots = mm("ecf,edf->ecd", pre_grad, my_in)
+        part_slots = mm("ecf,efd->ecd", after(hidden, *last), my_out)
+        cut_at = units * 2 // 3
+        dispatch_pair = mm("ecd,dk->eck", dispatch, pair_order).astype(BF16)
+        dispatch_line = mm("ecd,dk->eck", dispatch, line_order).astype(BF16)
+        in_first = dispatch_pair, pre_grad[:, :, : cut_at // 2]
+        in_second = dispatch_pair, pre_grad[:, :, cut_at // 2 : cut_at]
+        in_third = dispatch_line, pre_grad[:, :, cut_at:]
+        expert_part = to_tokens(part_slots)
+        back_part = to_tokens(back_slots)
+        state_z = None, swap(ready(sent_part(in_third)), 1 << LINE)
+        gate_part = jnp.sum(grad_seed * expert_part, axis=1)
+        gate_rows = jnp.pad(gate_part.reshape(-1, count // 4), ((0, 4), (0, width - count // 4)))
+        back = ready(jnp.concatenate([back_part, gate_rows], axis=0))
+        back_got = mp_other(back)
+        got_b = swap(ready(sent_part(out_second)), PAIR)
+        state_z = line_next((grads(in_third[0][:, :, mine], in_third[1]), state_z[1]))
+        state_a = begin(paired(out_first, got_a), LINE)
+        back_sum = back + take(back_got)
+        expert_back = back_sum[:count]
+        gate_grad = back_sum[count : count + 4, : count // 4].reshape(count, 1)
 
         logit_grad = (gate_grad * gate * (picked - router)).astype(BF16)
         grad_router = mm("td,te->de", normed_two, logit_grad)
@@ -228,7 +251,6 @@
         middle_grad, grad_gain_two = second_pull(second_grad)
         middle_grad = middle_grad + grad_seed
         attn_grad = middle_grad.astype(BF16)
-        grad_output_rows = mm("td,tc->dc", attn_grad, context)
         context_grad = (
             mm("td,cd->tc", attn_grad, w_output).astype(BF16).reshape(count, heads, HEAD)
         )
@@ -247,35 +269,74 @@
             + mm("tc,dc->td", key_grad, w_key)
             + mm("tc,dc->td", value_grad, w_value)
         )
-        first_grad = mp_sum(first_part)
-        grad_query_rows = mm("td,tc->dc", normed, query_grad)
-        grad_key_rows = mm("td,tc->dc", normed, key_grad)
-        grad_value_rows = mm("td,tc->dc", normed, value_grad)
-        dense = dense_sum(
-            jnp.concatenate(
-                [grad_query_rows, grad_key_rows, grad_value_rows, grad_output_rows], axis=1
-            )
-        )
+        first_part = ready(first_part)
+        first_got = mp_other(first_part)
+        got_c = swap(ready(sent_part(in_first)), PAIR)
+        state_a = line_next(state_a)
+        rows_z = finish(state_z)
+        qkv_grad = jnp.concatenate([query_grad, key_grad, value_grad], axis=1)
+        normed_core = mm("td,dk->tk", normed, core_order).astype(BF16)
+        attn_grad_core = mm("td,dk->tk", attn_grad, core_order).astype(BF16)
         _, first_pull = jax.vjp(norm_rows, inputs, gain_one)
+
+        def dense_first(columns):
+            return mm("td,tc->dc", normed_core[:, columns], qkv_grad)
+
+        state_b = begin(paired(out_second, got_b), LINE)
+        got_d = swap(ready(sent_part(in_second)), PAIR)
+        sums_a = core_begin(state_a)
+        first_grad = first_part + take(first_got)
+        gain_part = ready(first_pull(first_part)[1])
+        grad_gain_one = gain_part + take(mp_other(gain_part))
+        core_e = swap(ready(dense_first(other)), 1)
+        state_b = line_next(state_b)
+        own_e = (dense_first(mine) + take(core_e))[None]
+
+        table_rows = jnp.tile(grad_table.reshape(share, -1), (n_dp, 1))
+        small = jnp.concatenate(
+            [grad_gain_one[:, None], grad_gain_two[:, None], grad_router, table_rows], axis=1
+        )
+        n_small = small.shape[1]
+        small = jnp.pad(small, ((0, 0), (0, -n_small % 128)))
+        small = mm("dk,dc->kc", core_order.astype(F32), small, lax.Precision.HIGHEST)
+
+        def dense_second(columns):
+            product = mm("td,tc->dc", attn_grad_core[:, columns], context)
+            return jnp.concatenate([product, small[columns]], axis=1)
+
+        core_f = swap(ready(dense_second(other)), 1)
+        state_c = begin(paired(in_first, got_c), LINE)
+        state_e = begin(own_e, 1)
+        own_f = (dense_second(mine) + take(core_f))[None]
+        expert_got = mp_other(ready(expert_part))
+        state_c = line_next(state_c)
+        sums_b = core_begin(state_b)
+        state_d = begin(paired(in_second, got_d), LINE)
+        state_f = begin(own_f, 1)
+        state_z = begin(rows_z, 1)
+        sums_c = core_begin(state_c)
+        state_e = begin(finish(state_e), LINE)
+        state_d = line_next(state_d)
+        state_f = begin(finish(state_f), LINE)
+        expert_full = expert_part + take(expert_got)
+        mixed = (middle + gate * expert_full).astype(BF16)
+        state_e = line_next(state_e)
+        sums_z = core_begin(state_z)
+        state_f = line_next(state_f)
+        sums_d = core_begin(state_d)
+        qkv_sum = finish(state_e)[0]
+        last_sum = finish(state_f)[0]
+        output_sum = last_sum[:, :inner]
+        small = last_sum[:, inner : inner + n_small]
+        out_sums = [jnp.concatenate(pair, axis=0) for pair in zip(sums_a, sums_b)]
+        in_sums = [jnp.concatenate(three, axis=2) for three in zip(sums_c, sums_d, sums_z)]
+
         input_grad, _ = first_pull(first_grad)
         grad_tokens = middle_grad + input_grad
-        grad_gain_one = mp_sum(first_pull(first_part)[1])
-        small = jnp.concatenate(
-            [
-                grad_gain_one[None],
-                grad_gain_two[None],
-                grad_router.T,
-                jnp.pad(grad_table.T, ((0, 0), (0, width - NB))),
-            ],
-            axis=0,
-        )
-        small = dp_sum(small)
-        table_total = small[2 + E :, :NB].T
-        small = lax.dynamic_slice_in_dim(small[: 2 + E], device * share, share, 1)
+        table_total = small[:, 2 + E :].reshape(NB, heads)
 
         def by_expert(sums):
-            mine = jnp.stack([own for own, _ in sums])
-            other = jnp.stack([got for _, got in sums])
+            mine, other = sums
             first = core == 0
             return jnp.concatenate(
                 [jnp.where(first, mine, other), jnp.where(first, other, mine)], axis=0
@@ -284,14 +345,14 @@
         return (
             mixed,
             grad_tokens,
-            small[0],
-            dense[:, :inner],
-            dense[:, inner : 2 * inner],
-            dense[:, 2 * inner : 3 * inner],
-            dense[:, 3 * inner :].T,
+            small[:, 0],
+            qkv_sum[:, :inner],
+            qkv_sum[:, inner : 2 * inner],
+            qkv_sum[:, 2 * inner :],
+            output_sum.T,
             table_total,
-            small[1],
-            small[2:].T,
+            small[:, 1],
+            small[:, 2 : 2 + E],
             by_expert(in_sums),
             jnp.swapaxes(by_expert(out_sums), 1, 2),
         )

time: 588 us -> 367 us (0.62)
  waiting for transfers between devices: 313 us -> 190 us
  starting transfers between devices: 114 us -> 34.7 us
  local copies, waits for them, and re-layouts: 42.1 us -> 16.6 us
  matrix products: 71 us -> 85.8 us
  other arithmetic: 38.2 us -> 30.6 us
    ppermute x30 -> x0, starting transfers between devices: 88.8 us -> none  [flow(): lax.ppermute(piece, 'dp', [(a * block + k, b * block + k) for a, b in hop...]
    ppermute x30 -> x0, waiting for transfers between devices: 88.5 us -> none  [flow(): lax.ppermute(piece, 'dp', [(a * block + k, b * block + k) for a, b in hop...]
    ppermute x20 -> x34, waiting for transfers between devices: 189 us -> 158 us  [swap(): return lax.ppermute(value, 'dp', [(i, i ^ stride) for i in range(n_dp)])]
    dot_general x33 -> x47, matrix products: 71 us -> 85.8 us  [mm(): jnp.einsum(spec, left, right, preferred_element_type=F32, precision=preci...]
    squeeze x12 -> x1, local copies, waits for them, and re-layouts: 14.1 us -> 0.52 us  [shards(): small[:, 1]]
    ppermute x20 -> x34, starting transfers between devices: 15.2 us -> 26.5 us  [swap(): return lax.ppermute(value, 'dp', [(i, i ^ stride) for i in range(n_dp)])]
    add x31 -> x19, other arithmetic: 13.4 us -> 5.87 us  [the longest x14 5.62 us: finish(): return kept + take(got)]
    concatenate x1 -> x2, local copies, waits for them, and re-layouts: 6.07 us -> 0.04 us  [the longest x1 0.02 us: shards(): out_sums = [jnp.concatenate(pair, axis=0) for pair in zip(sums_a, sums_b)]]
  transfers between devices with their start and end apart: 56 -> 39, of which waited for: 25 -> 15; matrix products, arithmetic and copies ran while one was open for 18% -> 26% of each run, Pallas kernels for 0% -> 0%
where the time goes in v3:
time: 367 us; the launch traced here: 360 us
  waiting for transfers between devices  190 us (52%)
  matrix products  85.8 us (23%)
  starting transfers between devices  34.7 us (9%)
  other arithmetic  30.6 us (8%)
  local copies, waits for them, and re-layouts  16.6 us (5%)
    ppermute x34, waiting for transfers between devices, swap(): return lax.ppermute(value, 'dp', [(i, i ^ stride) for i in range(n_dp)])  158 us
    dot_general x47, matrix products, mm(): jnp.einsum(spec, left, right, preferred_element_type=F32, precision=preci...  85.8 us
    ppermute x5, waiting for transfers between devices, mp_other(): return lax.ppermute(value, 'mp', [(0, 1), (1, 0)])  32.5 us
    ppermute x34, starting transfers between devices, swap(): return lax.ppermute(value, 'dp', [(i, i ^ stride) for i in range(n_dp)])  26.5 us
    unnamed x133, local copies, waits for them, and re-layouts  9.11 us
    ppermute x5, starting transfers between devices, mp_other(): return lax.ppermute(value, 'mp', [(0, 1), (1, 0)])  8.21 us
  transfers between devices with their start and end apart: 39, of which 15 were waited for; matrix products, arithmetic and copies ran while one was open for 26% of the time, Pallas kernels for 0%

profile of v3, /device:TPU:0, one launch (start us, length us, event | category | flops | bytes accessed | tf_op | source)
XLA Modules:
  0.0 360.3 jit_solution(11941210482725020500)
XLA Ops:
  7.1 5.1 %fusion.1 = f32[512,512,6]{0,2,1:T(8,128)S(1)} fusion(s32[512,512]{0,1:T(8,128)S(1)} %fusion.70, bf16[32,6]{0,1:T(8,128)(2,1)S(1)} %copy-done.57), kind=kOutput, calls=%fused_computation.2 | convolution fusion | flops 109051904 | bytes 7340416 | tf_op jit(solution)/shard_map/qkb,bh->hqk/dot_general | solution.py:47
  12.2 4.9 %fusion.174 = (f32[6,512]{1,0:T(8,128)S(1)}, f32[6,512,512]{1,2,0:T(8,128)S(1)}) fusion(f32[512,512,6]{0,2,1:T(8,128)S(1)} %fusion.1, bf16[512,6,64]{0,2,1:T(8,128)(2,1)S(1)} %bitcast.160, bf16[512,6,64]{0,2,1:T(8,128)(2,1)S(1)} %bitcast.162, pred[512,512]{0,1:T(8,128)(4,1)S(1)} %broadcast_compare_fusion), kind=kOutput, calls=%fused_computation.287 | convolution fusion | flops 206042112 | bytes 13643776 | tf_op jit(solution)/shard_map/qhd,khd->hqk/dot_general | solution.py:47
  21.6 3.0 collective-permute-start
  26.8 32.3 %collective-permute-done = f32[512,768]{1,0:T(8,128)} collective-permute-done((f32[512,768]{1,0:T(8,128)S(1)}, f32[512,768]{1,0:T(8,128)}, u32[]{:S(2)}, u32[]{:S(2)}) %collective-permute-start) | collective-permute-done | bytes 1572896 | tf_op jit(solution)/shard_map/ppermute | solution.py:58
  75.0 4.1 %multiply_convert_fusion.1 = (bf16[2,320,1536]{2,1,0:T(8,128)(2,1)S(1)}, f32[2,320,1536]{2,1,0:T(8,128)S(1)}) fusion(bf16[4,768,1536]{2,1,0:T(8,128)(2,1)} %param.23, s32[]{:T(128)S(6)} %select_n.155, bf16[2,160,768]{2,1,0:T(8,128)(2,1)S(1)} %bitcast.168, bf16[2,160,768]{2,1,0:T(8,128)(2,1)S(1)} %bitcast.165), kind=kOutput, calls=%fused_computation.30 | convolution fusion | flops 1520762880 | bytes 11599876 | tf_op jit(solution)/shard_map/ecd,edf->ecf/dot_general | solution.py:47
  81.7 7.1 %fusion.21 = bf16[2,320,1536]{2,1,0:T(8,128)(2,1)S(1)} fusion(f32[2,320,1536]{2,1,0:T(8,128)S(1)} %get-tuple-element.228, bf16[2,320,768]{2,1,0:T(8,128)(2,1)S(1)} %pad_maximum_fusion.5, bf16[4,1536,768]{2,1,0:T(8,128)(2,1)} %param.24, s32[]{:T(128)S(6)} %select_n.155), kind=kOutput, calls=%fused_computation.29 | convolution fusion | flops 1529610240 | bytes 11599876 | tf_op jit(solution)/shard_map/ecd,efd->ecf/dot_general | solution.py:47
  90.9 4.0 %fusion.9 = f32[2,320,768]{2,1,0:T(8,128)S(1)} fusion(bf16[2,320,1536]{2,1,0:T(8,128)(2,1)S(1)} %get-tuple-element.72, bf16[4,1536,768]{2,1,0:T(8,128)(2,1)} %param.24, s32[]{:T(128)S(6)} %select_n.155), kind=kOutput, calls=%fused_computation.17 | convolution fusion | flops 1509949440 | bytes 8650756 | tf_op jit(solution)/shard_map/ecf,efd->ecd/dot_general | solution.py:47
  101.8 2.8 fusion.42
  114.0 19.5 %collective-permute-done.9 = f32[2,384,512]{2,1,0:T(8,128)S(1)} collective-permute-done((f32[2,384,512]{2,1,0:T(8,128)S(1)}, f32[2,384,512]{2,1,0:T(8,128)S(1)}, u32[]{:S(2)}, u32[]{:S(2)}) %collective-permute-start.9) | collective-permute-done | bytes 1572896 | tf_op jit(solution)/shard_map/ppermute | solution.py:55
  135.2 2.6 collective-permute-start.14
  159.7 7.8 %fusion.67 = f32[32,6]{1,0:T(8,128)S(1)} fusion(bf16[6,512,512]{1,2,0:T(8,128)(2,1)} %copy-done.3, s32[512,512]{0,1:T(8,128)} %copy-done.15), kind=kOutput, calls=%fused_computation.114 | convolution fusion | flops 109051904 | bytes 4195072 | tf_op jit(solution)/shard_map/hqk,qkb->bh/dot_general | solution.py:47
  167.5 16.5 %collective-permute-done.11 = f32[1,192,1536]{2,1,0:T(8,128)} collective-permute-done((f32[1,192,1536]{2,1,0:T(8,128)}, f32[1,192,1536]{2,1,0:T(8,128)}, u32[]{:S(2)}, u32[]{:S(2)}) %collective-permute-start.11) | collective-permute-done | bytes 1179680 | tf_op jit(solution)/shard_map/ppermute | solution.py:55
  187.6 2.8 fusion.26
  191.6 21.0 %collective-permute-done.12 = f32[1,96,1536]{2,1,0:T(8,128)S(1)} collective-permute-done((f32[1,96,1536]{2,1,0:T(8,128)S(1)}, f32[1,96,1536]{2,1,0:T(8,128)S(1)}, u32[]{:S(2)}, u32[]{:S(2)}) %collective-permute-start.12) | collective-permute-done | bytes 589856 | tf_op jit(solution)/shard_map/ppermute | solution.py:55
  213.6 2.7 fusion.45
  226.8 20.5 %collective-permute-done.17 = f32[1,192,1536]{2,1,0:T(8,128)} collective-permute-done((f32[1,192,1536]{2,1,0:T(8,128)}, f32[1,192,1536]{2,1,0:T(8,128)}, u32[]{:S(2)}, u32[]{:S(2)}) %collective-permute-start.17) | collective-permute-done | bytes 1179680 | tf_op jit(solution)/shard_map/ppermute | solution.py:55
  252.9 2.7 collective-permute-start.22
  259.9 23.8 %collective-permute-done.23 = f32[2,192,512]{2,1,0:T(8,128)S(1)} collective-permute-done((f32[2,192,512]{2,1,0:T(8,128)S(1)}, f32[2,192,512]{2,1,0:T(8,128)S(1)}, u32[]{:S(2)}, u32[]{:S(2)}) %collective-permute-start.23) | collective-permute-done | bytes 786464 | tf_op jit(solution)/shard_map/ppermute | solution.py:55
  289.3 14.4 %collective-permute-done.27 = f32[2,96,512]{2,1,0:T(8,128)S(1)} collective-permute-done((f32[2,96,512]{2,1,0:T(8,128)S(1)}, f32[2,96,512]{2,1,0:T(8,128)S(1)}, u32[]{:S(2)}, u32[]{:S(2)}) %collective-permute-start.27) | collective-permute-done | bytes 393248 | tf_op jit(solution)/shard_map/ppermute | solution.py:55
  306.6 9.3 %collective-permute-done.25 = f32[2,192,512]{2,1,0:T(8,128)S(1)} collective-permute-done((f32[2,192,512]{2,1,0:T(8,128)S(1)}, f32[2,192,512]{2,1,0:T(8,128)S(1)}, u32[]{:S(2)}, u32[]{:S(2)}) %collective-permute-start.25) | collective-permute-done | bytes 786464 | tf_op jit(solution)/shard_map/ppermute | solution.py:55
  318.6 9.4 %collective-permute-done.30 = f32[1,96,1152]{2,1,0:T(8,128)S(1)} collective-permute-done((f32[1,96,1152]{2,1,0:T(8,128)S(1)}, f32[1,96,1152]{2,1,0:T(8,128)S(1)}, u32[]{:S(2)}, u32[]{:S(2)}) %collective-permute-start.30) | collective-permute-done | bytes 442400 | tf_op jit(solution)/shard_map/ppermute | solution.py:55
  328.4 10.5 %collective-permute-done.28 = f32[1,96,512]{1,2,0:T(8,128)S(1)} collective-permute-done((f32[1,96,512]{1,2,0:T(8,128)S(1)}, f32[1,96,512]{1,2,0:T(8,128)S(1)}, u32[]{:S(2)}, u32[]{:S(2)}) %collective-permute-start.28) | collective-permute-done | bytes 196640 | tf_op jit(solution)/shard_map/ppermute | solution.py:55
  339.0 8.8 %collective-permute-done.33 = f32[2,96,512]{2,1,0:T(8,128)S(1)} collective-permute-done((f32[2,96,512]{2,1,0:T(8,128)S(1)}, f32[2,96,512]{2,1,0:T(8,128)S(1)}, u32[]{:S(2)}, u32[]{:S(2)}) %collective-permute-start.33) | collective-permute-done | bytes 393248 | tf_op jit(solution)/shard_map/ppermute | solution.py:55
  348.0 4.0 %fusion.43 = (f32[512,768]{1,0:T(8,128)}, bf16[512,768]{1,0:T(8,128)(2,1)}) fusion(f32[512,768]{1,0:T(8,128)S(1)} %copy-done.6, bf16[512,768]{1,0:T(8,128)(2,1)S(1)} %copy-done.7, f32[512]{0:T(512)S(1)} %multiply_multiply_fusion.2, f32[512]{0:T(512)S(1)} %fusion.140, f32[768]{0:T(1024)S(1)} %convert_element_type.189, f32[512,768]{1,0:T(8,128)} %add_add_fusion.2, ...), kind=kLoop, calls=%fused_computation.69 | loop fusion | flops 4718592 | bytes 12592128 | tf_op jit(solution)/shard_map/add | solution.py:335
  (334 shorter events, 118.4 us)
Async XLA Ops:
  21.6 37.5 %collective-permute-start = (f32[512,768]{1,0:T(8,128)S(1)}, f32[512,768]{1,0:T(8,128)}, u32[]{:S(2)}, u32[]{:S(2)}) collective-permute-start(f32[512,768]{1,0:T(8,128)S(1)} %fusion.176), channel_id=1, source_target_pairs={{0,1},{1,0},{2,3},{3,2},{4,5},{5,4},{6,7},{7,6},{8,9},{9,8},{10,11... | collective-permute-start | bytes 4718600 | tf_op jit(solution)/shard_map/ppermute | solution.py:58
  79.9 57.9 %collective-permute-start.8 = (f32[1,384,1536]{2,1,0:T(8,128)S(1)}, f32[1,384,1536]{2,1,0:T(8,128)S(1)}, u32[]{:S(2)}, u32[]{:S(2)}) collective-permute-start(f32[1,384,1536]{2,1,0:T(8,128)S(1)} %convolution_bitcast_fusion.3), channel_id=1, source_target_pairs={{0,4},{2,6},{4,0},{6,2},{8,12},{10,14},{12,8},{14,10},{16,20},{18,... | collective-permute-start | bytes 7077896 | tf_op jit(solution)/shard_map/ppermute | solution.py:55
  97.2 36.4 %collective-permute-start.9 = (f32[2,384,512]{2,1,0:T(8,128)S(1)}, f32[2,384,512]{2,1,0:T(8,128)S(1)}, u32[]{:S(2)}, u32[]{:S(2)}) collective-permute-start(f32[2,384,512]{2,1,0:T(8,128)S(1)} %fusion.97), channel_id=1, source_target_pairs={{0,8},{2,10},{4,12},{6,14},{8,0},{10,2},{12,4},{14,6},{16,24},{18,... | collective-permute-start | bytes 4718600 | tf_op jit(solution)/shard_map/ppermute | solution.py:55
  104.7 38.1 %collective-permute-start.7 = (f32[520,768]{1,0:T(8,128)S(1)}, f32[520,768]{1,0:T(8,128)S(1)}, u32[]{:S(2)}, u32[]{:S(2)}) collective-permute-start(f32[520,768]{1,0:T(8,128)S(1)} %select_maximum_fusion), channel_id=1, source_target_pairs={{0,1},{1,0},{2,3},{3,2},{4,5},{5,4},{6,7},{7,6},{8,9},{9,8},{10,11... | collective-permute-start | bytes 4792328 | tf_op jit(solution)/shard_map/ppermute | solution.py:58
  113.1 74.4 %collective-permute-start.13 = (f32[1,384,1536]{2,1,0:T(8,128)}, f32[1,384,1536]{2,1,0:T(8,128)}, u32[]{:S(2)}, u32[]{:S(2)}) collective-permute-start(f32[1,384,1536]{2,1,0:T(8,128)} %convolution_bitcast_fusion.1), channel_id=1, source_target_pairs={{0,4},{2,6},{4,0},{6,2},{8,12},{10,14},{12,8},{14,10},{16,20},{18,... | collective-permute-start | bytes 7077896 | tf_op jit(solution)/shard_map/ppermute | solution.py:55
  135.2 52.3 %collective-permute-start.14 = (f32[2,192,512]{2,1,0:T(8,128)}, f32[2,192,512]{2,1,0:T(8,128)}, u32[]{:S(2)}, u32[]{:S(2)}) collective-permute-start(f32[2,192,512]{2,1,0:T(8,128)} %slice.361), channel_id=1, source_target_pairs={{0,16},{2,18},{4,20},{6,22},{8,24},{10,26},{12,28},{14,30},{16,0},... | collective-permute-start | bytes 2359304 | tf_op jit(solution)/shard_map/ppermute | solution.py:55
  141.2 42.8 %collective-permute-start.11 = (f32[1,192,1536]{2,1,0:T(8,128)}, f32[1,192,1536]{2,1,0:T(8,128)}, u32[]{:S(2)}, u32[]{:S(2)}) collective-permute-start(f32[1,192,1536]{2,1,0:T(8,128)} %slice.362), channel_id=1, source_target_pairs={{0,8},{2,10},{4,12},{6,14},{8,0},{10,2},{12,4},{14,6},{16,24},{18,... | collective-permute-start | bytes 3538952 | tf_op jit(solution)/shard_map/ppermute | solution.py:55
  157.1 56.5 %collective-permute-start.10 = (f32[512,768]{1,0:T(8,128)}, f32[512,768]{1,0:T(8,128)}, u32[]{:S(2)}, u32[]{:S(2)}) collective-permute-start(f32[512,768]{1,0:T(8,128)} %add_add_fusion.2), channel_id=1, source_target_pairs={{0,1},{1,0},{2,3},{3,2},{4,5},{5,4},{6,7},{7,6},{8,9},{9,8},{10,11... | collective-permute-start | bytes 4718600 | tf_op jit(solution)/shard_map/ppermute | solution.py:58
  158.6 90.3 %collective-permute-start.19 = (f32[2,384,512]{2,1,0:T(8,128)}, f32[2,384,512]{2,1,0:T(8,128)}, u32[]{:S(2)}, u32[]{:S(2)}) collective-permute-start(f32[2,384,512]{2,1,0:T(8,128)} %fusion.94), channel_id=1, source_target_pairs={{0,4},{2,6},{4,0},{6,2},{8,12},{10,14},{12,8},{14,10},{16,20},{18,... | collective-permute-start | bytes 4718600 | tf_op jit(solution)/shard_map/ppermute | solution.py:55
  185.8 26.8 %collective-permute-start.12 = (f32[1,96,1536]{2,1,0:T(8,128)S(1)}, f32[1,96,1536]{2,1,0:T(8,128)S(1)}, u32[]{:S(2)}, u32[]{:S(2)}) collective-permute-start(f32[1,96,1536]{2,1,0:T(8,128)S(1)} %slice.370), channel_id=1, source_target_pairs={{0,16},{2,18},{4,20},{6,22},{8,24},{10,26},{12,28},{14,30},{16,0},... | collective-permute-start | bytes 1769480 | tf_op jit(solution)/shard_map/ppermute | solution.py:55
  219.8 27.5 %collective-permute-start.17 = (f32[1,192,1536]{2,1,0:T(8,128)}, f32[1,192,1536]{2,1,0:T(8,128)}, u32[]{:S(2)}, u32[]{:S(2)}) collective-permute-start(f32[1,192,1536]{2,1,0:T(8,128)} %slice.373), channel_id=1, source_target_pairs={{0,8},{2,10},{4,12},{6,14},{8,0},{10,2},{12,4},{14,6},{16,24},{18,... | collective-permute-start | bytes 3538952 | tf_op jit(solution)/shard_map/ppermute | solution.py:55
  219.9 28.9 %collective-permute-start.16 = (f32[384,1152]{1,0:T(8,128)}, f32[384,1152]{1,0:T(8,128)}, u32[]{:S(2)}, u32[]{:S(2)}) collective-permute-start(f32[384,1152]{1,0:T(8,128)} %fusion.103), channel_id=1, source_target_pairs={{0,2},{2,0},{4,6},{6,4},{8,10},{10,8},{12,14},{14,12},{16,18},{18,... | collective-permute-start | bytes 5308424 | tf_op jit(solution)/shard_map/ppermute | solution.py:55
  224.3 60.3 %collective-permute-start.21 = (f32[2,384,512]{2,1,0:T(8,128)S(1)}, f32[2,384,512]{2,1,0:T(8,128)S(1)}, u32[]{:S(2)}, u32[]{:S(2)}) collective-permute-start(f32[2,384,512]{2,1,0:T(8,128)S(1)} %copy-done.42), channel_id=1, source_target_pairs={{0,4},{2,6},{4,0},{6,2},{8,12},{10,14},{12,8},{14,10},{16,20},{18,... | collective-permute-start | bytes 4718600 | tf_op jit(solution)/shard_map/ppermute | solution.py:55
  225.6 30.0 %collective-permute-start.37 = (f32[1,48,1536]{2,1,0:T(8,128)}, f32[1,48,1536]{2,1,0:T(8,128)S(1)}, u32[]{:S(2)}, u32[]{:S(2)}) collective-permute-start(f32[1,48,1536]{2,1,0:T(8,128)} %get-tuple-element.91), channel_id=1, source_target_pairs={{0,2},{2,0},{4,6},{6,4},{8,10},{10,8},{12,14},{14,12},{16,18},{18,... | collective-permute-start | bytes 884744 | tf_op jit(solution)/shard_map/ppermute | solution.py:55
  251.1 32.5 %collective-permute-start.23 = (f32[2,192,512]{2,1,0:T(8,128)S(1)}, f32[2,192,512]{2,1,0:T(8,128)S(1)}, u32[]{:S(2)}, u32[]{:S(2)}) collective-permute-start(f32[2,192,512]{2,1,0:T(8,128)S(1)} %slice.382), channel_id=1, source_target_pairs={{0,8},{2,10},{4,12},{6,14},{8,0},{10,2},{12,4},{14,6},{16,24},{18,... | collective-permute-start | bytes 2359304 | tf_op jit(solution)/shard_map/ppermute | solution.py:55
  252.9 31.5 %collective-permute-start.22 = (f32[1,96,1536]{2,1,0:T(8,128)S(1)}, f32[1,96,1536]{2,1,0:T(8,128)S(1)}, u32[]{:S(2)}, u32[]{:S(2)}) collective-permute-start(f32[1,96,1536]{2,1,0:T(8,128)S(1)} %slice.378), channel_id=1, source_target_pairs={{0,16},{2,18},{4,20},{6,22},{8,24},{10,26},{12,28},{14,30},{16,0},... | collective-permute-start | bytes 1769480 | tf_op jit(solution)/shard_map/ppermute | solution.py:55
  258.0 47.0 %collective-permute-start.26 = (f32[1,192,1152]{2,1,0:T(8,128)S(1)}, f32[1,192,1152]{2,1,0:T(8,128)S(1)}, u32[]{:S(2)}, u32[]{:S(2)}) collective-permute-start(f32[1,192,1152]{2,1,0:T(8,128)S(1)} %slice.380), channel_id=1, source_target_pairs={{0,4},{2,6},{4,0},{6,2},{8,12},{10,14},{12,8},{14,10},{16,20},{18,... | collective-permute-start | bytes 2654216 | tf_op jit(solution)/shard_map/ppermute | solution.py:55
  259.4 59.2 %collective-permute-start.20 = (f32[512,768]{1,0:T(8,128)S(1)}, f32[512,768]{1,0:T(8,128)S(1)}, u32[]{:S(2)}, u32[]{:S(2)}) collective-permute-start(f32[512,768]{1,0:T(8,128)S(1)} %copy-done.17), channel_id=1, source_target_pairs={{0,1},{1,0},{2,3},{3,2},{4,5},{5,4},{6,7},{7,6},{8,9},{9,8},{10,11... | collective-permute-start | bytes 4718600 | tf_op jit(solution)/shard_map/ppermute | solution.py:58
  285.4 30.8 %collective-permute-start.24 = (f32[1,192,512]{1,2,0:T(8,128)S(1)}, f32[1,192,512]{1,2,0:T(8,128)S(1)}, u32[]{:S(2)}, u32[]{:S(2)}) collective-permute-start(f32[1,192,512]{1,2,0:T(8,128)S(1)} %slice.386), channel_id=1, source_target_pairs={{0,4},{2,6},{4,0},{6,2},{8,12},{10,14},{12,8},{14,10},{16,20},{18,... | collective-permute-start | bytes 1179656 | tf_op jit(solution)/shard_map/ppermute | solution.py:55
  286.8 29.1 %collective-permute-start.25 = (f32[2,192,512]{2,1,0:T(8,128)S(1)}, f32[2,192,512]{2,1,0:T(8,128)S(1)}, u32[]{:S(2)}, u32[]{:S(2)}) collective-permute-start(f32[2,192,512]{2,1,0:T(8,128)S(1)} %slice.391), channel_id=1, source_target_pairs={{0,8},{2,10},{4,12},{6,14},{8,0},{10,2},{12,4},{14,6},{16,24},{18,... | collective-permute-start | bytes 2359304 | tf_op jit(solution)/shard_map/ppermute | solution.py:55
  303.7 24.5 %collective-permute-start.29 = (f32[2,96,512]{2,1,0:T(8,128)S(1)}, f32[2,96,512]{2,1,0:T(8,128)S(1)}, u32[]{:S(2)}, u32[]{:S(2)}) collective-permute-start(f32[2,96,512]{2,1,0:T(8,128)S(1)} %slice.396), channel_id=1, source_target_pairs={{0,4},{2,6},{4,0},{6,2},{8,12},{10,14},{12,8},{14,10},{16,20},{18,... | collective-permute-start | bytes 1179656 | tf_op jit(solution)/shard_map/ppermute | solution.py:55
  316.1 31.7 %collective-permute-start.33 = (f32[2,96,512]{2,1,0:T(8,128)S(1)}, f32[2,96,512]{2,1,0:T(8,128)S(1)}, u32[]{:S(2)}, u32[]{:S(2)}) collective-permute-start(f32[2,96,512]{2,1,0:T(8,128)S(1)} %slice.399), channel_id=1, source_target_pairs={{0,16},{2,18},{4,20},{6,22},{8,24},{10,26},{12,28},{14,30},{16,0},... | collective-permute-start | bytes 1179656 | tf_op jit(solution)/shard_map/ppermute | solution.py:55
  328.1 26.4 %collective-permute-start.32 = (f32[1,48,1152]{2,1,0:T(8,128)S(1)}, f32[1,48,1152]{2,1,0:T(8,128)S(1)}, u32[]{:S(2)}, u32[]{:S(2)}) collective-permute-start(f32[1,48,1152]{2,1,0:T(8,128)S(1)} %slice.404), channel_id=1, source_target_pairs={{0,16},{2,18},{4,20},{6,22},{8,24},{10,26},{12,28},{14,30},{16,0},... | collective-permute-start | bytes 663560 | tf_op jit(solution)/shard_map/ppermute | solution.py:55
  328.3 23.7 %collective-permute-start.36 = (f32[2,48,512]{2,1,0:T(8,128)S(1)}, f32[2,48,512]{2,1,0:T(8,128)S(1)}, u32[]{:S(2)}, u32[]{:S(2)}) collective-permute-start(f32[2,48,512]{2,1,0:T(8,128)S(1)} %get-tuple-element.125), channel_id=1, source_target_pairs={{0,2},{2,0},{4,6},{6,4},{8,10},{10,8},{12,14},{14,12},{16,18},{18,... | collective-permute-start | bytes 589832 | tf_op jit(solution)/shard_map/ppermute | solution.py:55
  (79 other events, 667.4 us)
